TPU v7x, 512 devices: a whole 4x8x8 slice. The times are simulated.
512 devices in a mesh: col: 64 (over z, x, core), mem: 8 (over y).
Axes of the slice: x: 4, y: 8, z: 8, core: 2. Of those that a mesh axis runs over, the one named last changes fastest.
Arguments:
- ensemble: bfloat16 [320, 393216], P('mem', 'col'), may hold values from -6 to 6
- control: bfloat16 [4, 393216], P(None, 'col'), may hold values from -6 to 6
- pair_home: int32 [16384, 1], replicated, may hold values from 0 to 63; in each aligned block of 256 rows (0 to 255, 256 to 511, ...) at most 5 rows name the same one
- pair_local: int32 [16384], replicated, may hold values from 0 to 23
- pair_count: int32 [64], P('col'), may hold values from 1 to 128, 5120 in all
- pair_shift: float32 [2, 8192], P(None, 'col'), may hold values from -410 to 410
Outputs:
- increment: float32 [4, 393216], P(None, ('col', 'mem'))
Inputs may be any that keep to these rules, and one draw needn't show every extreme that they name: `pair_home`: rows 2 (o * 128 + s) and 2 (o * 128 + s) + 1 name the home devices of the two blocks of owner o's slot s; among the 256 rows of one owner no device is named more than 5 times, and for some owner some device is named exactly 5 times. `pair_count`: the counts sum to the number of live pairs; the largest is exactly 128.
All inputs are finite; a program needn't handle non-finite values. No bound on the sum of `pair_count` on one device may be relied on, other than what follows from the above.
Results may differ from a plain program's by a relative error of at most 0.0048.
Values may be sent and summed in bfloat16 or wider, within the bound.
A program may use at most 64 MiB of HBM per device.

v0:
```python
import jax
import jax.numpy as jnp
from jax import lax
from jax.sharding import PartitionSpec as P

MEMBERS = 80
LEVELS = 4
BLOCK_SIDE = 16
PEER_CAP = 5
BLOCK = 256


SPACING_KM = 200.0
HALF_WIDTH = 250.0
GROUP_SLOTS = 16


def gaspari_cohn(distance):
    scaled = distance / HALF_WIDTH
    near_part = (
        ((-0.25 * scaled + 0.5) * scaled + 0.625) * scaled - 5.0 / 3.0
    ) * scaled * scaled + 1.0
    bounded = jnp.maximum(scaled, 1.0)
    far_part = (
        ((((scaled / 12.0 - 0.5) * scaled + 0.625) * scaled + 5.0 / 3.0) * scaled - 5.0) * scaled
        + 4.0
        - 2.0 / (3.0 * bounded)
    )
    return jnp.where(scaled <= 1.0, near_part, jnp.where(scaled <= 2.0, far_part, 0.0))


def taper_tiles(offsets, live_slot):
    lattice = jnp.arange(BLOCK_SIDE * BLOCK_SIDE)
    east_km = (lattice % BLOCK_SIDE).astype(jnp.float32) * SPACING_KM
    north_km = (lattice // BLOCK_SIDE).astype(jnp.float32) * SPACING_KM
    delta_east = offsets[0][:, None, None] + east_km[None, None, :] - east_km[None, :, None]
    delta_north = offsets[1][:, None, None] + north_km[None, None, :] - north_km[None, :, None]
    taper = gaspari_cohn(jnp.sqrt(delta_east * delta_east + delta_north * delta_north))
    return (taper * live_slot[:, None, None]).astype(jnp.bfloat16)


def pair_results(taper, first_side, second_side):
    to_first = jnp.einsum("spq,smq->smp", taper, second_side, preferred_element_type=jnp.float32)
    to_second = jnp.einsum("spq,smp->smq", taper, first_side, preferred_element_type=jnp.float32)
    return jnp.stack((to_first.astype(jnp.bfloat16), to_second.astype(jnp.bfloat16)), axis=1)


def grouped(pieces, offsets, live_slot, finish):
    slot_count = offsets.shape[1]
    groups = -(-slot_count // GROUP_SLOTS)

    def split_rows(leaf_array):
        return leaf_array.reshape((groups, GROUP_SLOTS) + leaf_array.shape[1:])

    offset_parts = offsets.reshape(2, groups, GROUP_SLOTS).transpose(1, 0, 2)

    def one_group(inputs):
        inputs_part, part_offsets, part_live = inputs
        return finish(taper_tiles(part_offsets, part_live), inputs_part)

    outcome = lax.map(one_group, (split_rows(pieces), offset_parts, split_rows(live_slot)))
    return outcome.reshape((groups * GROUP_SLOTS,) + outcome.shape[2:])


def shards(ensemble, control, pair_home, pair_local, pair_count, pair_shift):
    owners = lax.axis_size("col")
    own_index = lax.axis_index("col")
    member_rows = ensemble.shape[0]
    columns = ensemble.shape[1]
    blocks = columns // BLOCK
    slot_count = pair_shift.shape[1]
    requests = 2 * slot_count
    peer_ids = jnp.arange(owners)
    level_of = (lax.axis_index("mem") * member_rows + jnp.arange(member_rows)) // MEMBERS
    level_hot = (level_of[:, None] == jnp.arange(LEVELS)[None, :]).astype(jnp.float32)
    home_rows = pair_home.reshape(owners, requests)
    local_block = pair_local.reshape(owners, requests)
    from_here = (home_rows == own_index).astype(jnp.int32)
    rank_here = jnp.cumsum(from_here, axis=1) - from_here
    place_index = jnp.arange(PEER_CAP)
    matched = from_here[:, :, None] * (rank_here[:, :, None] == place_index[None, None, :]).astype(
        jnp.int32
    )
    chosen = jnp.sum(matched * local_block[:, :, None], axis=1).reshape(owners * PEER_CAP)
    filled = jnp.sum(matched, axis=1).reshape(owners * PEER_CAP)
    own_homes = lax.dynamic_index_in_dim(home_rows, own_index, 0, keepdims=False)
    own_hot = (own_homes[:, None] == peer_ids[None, :]).astype(jnp.int32)
    own_rank = jnp.sum((jnp.cumsum(own_hot, axis=0) - own_hot) * own_hot, axis=1)
    position = own_homes * PEER_CAP + own_rank
    live_slot = (jnp.arange(slot_count) < pair_count[0]).astype(jnp.float32)
    collect = (chosen[None, :] == jnp.arange(blocks)[:, None]).astype(jnp.int32) * filled[None, :]
    ensemble_blocks = ensemble.reshape(member_rows, blocks, BLOCK)
    control_blocks = control.reshape(LEVELS, blocks, BLOCK)
    spread = jnp.einsum(
        "ml,lbc->mbc",
        level_hot,
        control_blocks.astype(jnp.float32),
        precision=lax.Precision.HIGHEST,
    )
    weighted = (
        (ensemble_blocks.astype(jnp.float32) * spread).astype(jnp.bfloat16).transpose(1, 0, 2)
    )
    outgoing = jnp.take(weighted, chosen, axis=0)
    arrived = lax.all_to_all(outgoing, "col", split_axis=0, concat_axis=0, tiled=True)
    pieces = jnp.take(arrived, position, axis=0).reshape(slot_count, 2, member_rows, BLOCK)

    def finish(taper, inputs_part):
        return pair_results(taper, inputs_part[:, 0], inputs_part[:, 1])

    results = grouped(pieces, pair_shift, live_slot, finish).reshape(requests, member_rows, BLOCK)
    returned = (
        jnp.zeros((owners * PEER_CAP, member_rows, BLOCK), jnp.bfloat16).at[position].set(results)
    )
    received = lax.all_to_all(returned, "col", split_axis=0, concat_axis=0, tiled=True)
    accumulated = jnp.einsum(
        "be,emc->bmc", collect.astype(jnp.bfloat16), received, preferred_element_type=jnp.float32
    )
    partial_sums = jnp.einsum(
        "ml,mbc,bmc->lbc",
        level_hot,
        ensemble_blocks.astype(jnp.float32),
        accumulated,
        precision=lax.Precision.HIGHEST,
    )
    partial_sums = partial_sums.reshape(LEVELS, columns)
    summed = lax.psum_scatter(partial_sums, "mem", scatter_dimension=1, tiled=True)
    return summed / (MEMBERS - 1.0)


def solution(mesh):
    return jax.shard_map(
        shards,
        mesh=mesh,
        in_specs=(P("mem", "col"), P(None, "col"), P(), P(), P("col"), P(None, "col")),
        out_specs=P(None, ("col", "mem")),
        check_vma=False,
    )
```

profile of v0, /device:TPU:1, one launch (start us, length us, event | category | flops | bytes accessed | tf_op | source)
XLA Modules:
  0.0 574.5 jit_solution(3800890114757897162)
XLA Ops:
  15.1 14.1 %gather_fusion = bf16[320,40,256]{2,1,0:T(8,128)(2,1)} fusion(bf16[24,40,256]{2,1,0:T(8,128)(2,1)S(1)} %fusion.61, s32[1024]{0:T(1024)S(1)} %pad_clamp_fusion.1), kind=kCustom, calls=%fused_computation | custom fusion | bytes 13108480 | tf_op jit(solution)/shard_map/jit(_take)/gather | solution.py:103
  29.2 7.1 %broadcast_select_fusion = bf16[320,40,256]{2,1,0:T(8,128)(2,1)} fusion(bf16[320,40,256]{2,1,0:T(8,128)(2,1)} %gather_fusion, pred[320]{0:T(512)(128)(4,1)S(1)} %compare_and_fusion.1), kind=kLoop, calls=%fused_computation.70 | loop fusion | flops 3276800 | bytes 13107520 | tf_op jit(solution)/shard_map/jit(_take)/select_n | solution.py:103
  36.3 15.2 %all-to-all-start = ((bf16[320,40,256]{2,1,0:T(8,128)(2,1)}), bf16[320,40,256]{2,1,0:T(8,128)(2,1)}, u32[]{:S(2)}, u32[]{:S(2)}) async-start(bf16[320,40,256]{2,1,0:T(8,128)(2,1)} %broadcast_select_fusion), calls=%async_computation | async-start | bytes 13107200 | tf_op jit(solution)/shard_map/all_to_all | solution.py:104
  53.8 141.6 %all-to-all-done = bf16[320,40,256]{2,1,0:T(8,128)(2,1)} async-done(((bf16[320,40,256]{2,1,0:T(8,128)(2,1)}), bf16[320,40,256]{2,1,0:T(8,128)(2,1)}, u32[]{:S(2)}, u32[]{:S(2)}) %all-to-all-start) | async-done | bytes 6553632 | tf_op jit(solution)/shard_map/all_to_all | solution.py:104
  195.4 6.1 %gather_fusion.1 = bf16[256,40,256]{2,1,0:T(8,128)(2,1)} fusion(bf16[320,40,256]{2,1,0:T(8,128)(2,1)} %all-to-all-done, s32[1024]{0:T(1024)S(1)} %pad_clamp_fusion), kind=kCustom, calls=%fused_computation.1 | custom fusion | bytes 10486784 | tf_op jit(solution)/shard_map/jit(_take)/gather | solution.py:105
  207.0 114.5 %while.12 = (s32[]{:T(128)}, bf16[8,16,2,40,256]{4,3,2,1,0:T(8,128)(2,1)}, bf16[8,16,2,40,256]{4,3,1,2,0:T(8,128)(2,1)}, f32[8,2,16]{2,0,1:T(8,128)S(1)}, f32[8,16]{1,0:T(8,128)S(1)}, /*index=5*/s32[]{:T(128)}) while((s32[]{:T(128)}, bf16[8,16,2,40,256]{4,3,2,1,0:T(8,128)(2,1)}, bf16[8,16,2,40,256]{4,3,1,2,0:T(8,128)(2,1)}, ...), condition=%wide.region_8.9_spmd, body=%wide.region_7.8_spmd.sunk | while | flops 241840128 | bytes 4041041 | solution.py:61
  208.3 6.0 %fusion.94 = bf16[16,1,40,256]{3,2,0,1:T(8,128)(2,1)S(1)} fusion(f32[16]{0:T(128)S(1)} %fusion.91, f32[256]{0:T(256)S(1)} %get-tuple-element.164, f32[16,256]{1,0:T(8,128)S(1)} %broadcast_add_fusion.4, f32[256]{0:T(256)S(1)} %get-tuple-element.166, f32[16,256]{1,0:T(8,128)S(1)} %broadcast_add_fusion.5, ...), kind=kOutput, calls=%fused_computation.17.clone.1 | convolution fusion | flops 120750080 | bytes 690688 | tf_op jit(solution)/shard_map/while/body/eval_jaxpr/spq,smq->smp/dot_general | solution.py:43
  214.3 6.1 %fusion.93 = bf16[16,1,40,256]{3,2,0,1:T(8,128)(2,1)S(1)} fusion(f32[16]{0:T(128)S(1)} %fusion.91, f32[256]{0:T(256)S(1)} %get-tuple-element.164, f32[16,256]{1,0:T(8,128)S(1)} %broadcast_add_fusion.4, f32[256]{0:T(256)S(1)} %get-tuple-element.166, f32[16,256]{1,0:T(8,128)S(1)} %broadcast_add_fusion.5, ...), kind=kOutput, calls=%fused_computation.16.clone.1 | convolution fusion | flops 120750080 | bytes 690688 | tf_op jit(solution)/shard_map/while/body/eval_jaxpr/spq,smp->smq/dot_general | solution.py:44
  222.6 6.0 %fusion.94 = bf16[16,1,40,256]{3,2,0,1:T(8,128)(2,1)S(1)} fusion(f32[16]{0:T(128)S(1)} %fusion.91, f32[256]{0:T(256)S(1)} %get-tuple-element.164, f32[16,256]{1,0:T(8,128)S(1)} %broadcast_add_fusion.4, f32[256]{0:T(256)S(1)} %get-tuple-element.166, f32[16,256]{1,0:T(8,128)S(1)} %broadcast_add_fusion.5, ...), kind=kOutput, calls=%fused_computation.17.clone.1 | convolution fusion | flops 120750080 | bytes 690688 | tf_op jit(solution)/shard_map/while/body/eval_jaxpr/spq,smq->smp/dot_general | solution.py:43
  228.6 6.1 %fusion.93 = bf16[16,1,40,256]{3,2,0,1:T(8,128)(2,1)S(1)} fusion(f32[16]{0:T(128)S(1)} %fusion.91, f32[256]{0:T(256)S(1)} %get-tuple-element.164, f32[16,256]{1,0:T(8,128)S(1)} %broadcast_add_fusion.4, f32[256]{0:T(256)S(1)} %get-tuple-element.166, f32[16,256]{1,0:T(8,128)S(1)} %broadcast_add_fusion.5, ...), kind=kOutput, calls=%fused_computation.16.clone.1 | convolution fusion | flops 120750080 | bytes 690688 | tf_op jit(solution)/shard_map/while/body/eval_jaxpr/spq,smp->smq/dot_general | solution.py:44
  236.9 6.0 %fusion.94 = bf16[16,1,40,256]{3,2,0,1:T(8,128)(2,1)S(1)} fusion(f32[16]{0:T(128)S(1)} %fusion.91, f32[256]{0:T(256)S(1)} %get-tuple-element.164, f32[16,256]{1,0:T(8,128)S(1)} %broadcast_add_fusion.4, f32[256]{0:T(256)S(1)} %get-tuple-element.166, f32[16,256]{1,0:T(8,128)S(1)} %broadcast_add_fusion.5, ...), kind=kOutput, calls=%fused_computation.17.clone.1 | convolution fusion | flops 120750080 | bytes 690688 | tf_op jit(solution)/shard_map/while/body/eval_jaxpr/spq,smq->smp/dot_general | solution.py:43
  243.0 6.1 %fusion.93 = bf16[16,1,40,256]{3,2,0,1:T(8,128)(2,1)S(1)} fusion(f32[16]{0:T(128)S(1)} %fusion.91, f32[256]{0:T(256)S(1)} %get-tuple-element.164, f32[16,256]{1,0:T(8,128)S(1)} %broadcast_add_fusion.4, f32[256]{0:T(256)S(1)} %get-tuple-element.166, f32[16,256]{1,0:T(8,128)S(1)} %broadcast_add_fusion.5, ...), kind=kOutput, calls=%fused_computation.16.clone.1 | convolution fusion | flops 120750080 | bytes 690688 | tf_op jit(solution)/shard_map/while/body/eval_jaxpr/spq,smp->smq/dot_general | solution.py:44
  251.2 6.0 %fusion.94 = bf16[16,1,40,256]{3,2,0,1:T(8,128)(2,1)S(1)} fusion(f32[16]{0:T(128)S(1)} %fusion.91, f32[256]{0:T(256)S(1)} %get-tuple-element.164, f32[16,256]{1,0:T(8,128)S(1)} %broadcast_add_fusion.4, f32[256]{0:T(256)S(1)} %get-tuple-element.166, f32[16,256]{1,0:T(8,128)S(1)} %broadcast_add_fusion.5, ...), kind=kOutput, calls=%fused_computation.17.clone.1 | convolution fusion | flops 120750080 | bytes 690688 | tf_op jit(solution)/shard_map/while/body/eval_jaxpr/spq,smq->smp/dot_general | solution.py:43
  257.3 6.1 %fusion.93 = bf16[16,1,40,256]{3,2,0,1:T(8,128)(2,1)S(1)} fusion(f32[16]{0:T(128)S(1)} %fusion.91, f32[256]{0:T(256)S(1)} %get-tuple-element.164, f32[16,256]{1,0:T(8,128)S(1)} %broadcast_add_fusion.4, f32[256]{0:T(256)S(1)} %get-tuple-element.166, f32[16,256]{1,0:T(8,128)S(1)} %broadcast_add_fusion.5, ...), kind=kOutput, calls=%fused_computation.16.clone.1 | convolution fusion | flops 120750080 | bytes 690688 | tf_op jit(solution)/shard_map/while/body/eval_jaxpr/spq,smp->smq/dot_general | solution.py:44
  265.6 6.0 %fusion.94 = bf16[16,1,40,256]{3,2,0,1:T(8,128)(2,1)S(1)} fusion(f32[16]{0:T(128)S(1)} %fusion.91, f32[256]{0:T(256)S(1)} %get-tuple-element.164, f32[16,256]{1,0:T(8,128)S(1)} %broadcast_add_fusion.4, f32[256]{0:T(256)S(1)} %get-tuple-element.166, f32[16,256]{1,0:T(8,128)S(1)} %broadcast_add_fusion.5, ...), kind=kOutput, calls=%fused_computation.17.clone.1 | convolution fusion | flops 120750080 | bytes 690688 | tf_op jit(solution)/shard_map/while/body/eval_jaxpr/spq,smq->smp/dot_general | solution.py:43
  271.6 6.1 %fusion.93 = bf16[16,1,40,256]{3,2,0,1:T(8,128)(2,1)S(1)} fusion(f32[16]{0:T(128)S(1)} %fusion.91, f32[256]{0:T(256)S(1)} %get-tuple-element.164, f32[16,256]{1,0:T(8,128)S(1)} %broadcast_add_fusion.4, f32[256]{0:T(256)S(1)} %get-tuple-element.166, f32[16,256]{1,0:T(8,128)S(1)} %broadcast_add_fusion.5, ...), kind=kOutput, calls=%fused_computation.16.clone.1 | convolution fusion | flops 120750080 | bytes 690688 | tf_op jit(solution)/shard_map/while/body/eval_jaxpr/spq,smp->smq/dot_general | solution.py:44
  279.8 6.0 %fusion.94 = bf16[16,1,40,256]{3,2,0,1:T(8,128)(2,1)S(1)} fusion(f32[16]{0:T(128)S(1)} %fusion.91, f32[256]{0:T(256)S(1)} %get-tuple-element.164, f32[16,256]{1,0:T(8,128)S(1)} %broadcast_add_fusion.4, f32[256]{0:T(256)S(1)} %get-tuple-element.166, f32[16,256]{1,0:T(8,128)S(1)} %broadcast_add_fusion.5, ...), kind=kOutput, calls=%fused_computation.17.clone.1 | convolution fusion | flops 120750080 | bytes 690688 | tf_op jit(solution)/shard_map/while/body/eval_jaxpr/spq,smq->smp/dot_general | solution.py:43
  285.9 6.1 %fusion.93 = bf16[16,1,40,256]{3,2,0,1:T(8,128)(2,1)S(1)} fusion(f32[16]{0:T(128)S(1)} %fusion.91, f32[256]{0:T(256)S(1)} %get-tuple-element.164, f32[16,256]{1,0:T(8,128)S(1)} %broadcast_add_fusion.4, f32[256]{0:T(256)S(1)} %get-tuple-element.166, f32[16,256]{1,0:T(8,128)S(1)} %broadcast_add_fusion.5, ...), kind=kOutput, calls=%fused_computation.16.clone.1 | convolution fusion | flops 120750080 | bytes 690688 | tf_op jit(solution)/shard_map/while/body/eval_jaxpr/spq,smp->smq/dot_general | solution.py:44
  300.2 6.1 %fusion.93 = bf16[16,1,40,256]{3,2,0,1:T(8,128)(2,1)S(1)} fusion(f32[16]{0:T(128)S(1)} %fusion.91, f32[256]{0:T(256)S(1)} %get-tuple-element.164, f32[16,256]{1,0:T(8,128)S(1)} %broadcast_add_fusion.4, f32[256]{0:T(256)S(1)} %get-tuple-element.166, f32[16,256]{1,0:T(8,128)S(1)} %broadcast_add_fusion.5, ...), kind=kOutput, calls=%fused_computation.16.clone.1 | convolution fusion | flops 120750080 | bytes 690688 | tf_op jit(solution)/shard_map/while/body/eval_jaxpr/spq,smp->smq/dot_general | solution.py:44
  314.5 6.1 %fusion.93 = bf16[16,1,40,256]{3,2,0,1:T(8,128)(2,1)S(1)} fusion(f32[16]{0:T(128)S(1)} %fusion.91, f32[256]{0:T(256)S(1)} %get-tuple-element.164, f32[16,256]{1,0:T(8,128)S(1)} %broadcast_add_fusion.4, f32[256]{0:T(256)S(1)} %get-tuple-element.166, f32[16,256]{1,0:T(8,128)S(1)} %broadcast_add_fusion.5, ...), kind=kOutput, calls=%fused_computation.16.clone.1 | convolution fusion | flops 120750080 | bytes 690688 | tf_op jit(solution)/shard_map/while/body/eval_jaxpr/spq,smp->smq/dot_general | solution.py:44
  324.6 34.3 %scatter_fusion = bf16[320,40,256]{2,1,0:T(8,128)(2,1)} fusion(bf16[320,40,256]{2,1,0:T(8,128)(2,1)} %broadcast_in_dim.54, s32[256]{0:T(256)S(1)} %bitcast.116, bf16[256,40,256]{2,1,0:T(8,128)(2,1)} %bitcast.23), kind=kCustom, calls=%fused_computation.2 | custom fusion | bytes 15729664 | tf_op jit(solution)/shard_map/scatter | solution.py:112
  358.9 8.9 %all-to-all-start.1 = ((bf16[320,40,256]{2,1,0:T(8,128)(2,1)}), bf16[320,40,256]{2,1,0:T(8,128)(2,1)}, u32[]{:S(2)}, u32[]{:S(2)}) async-start(bf16[320,40,256]{2,1,0:T(8,128)(2,1)} %scatter_fusion), calls=%async_computation.1 | async-start | bytes 13107200 | tf_op jit(solution)/shard_map/all_to_all | solution.py:114
  368.4 143.4 %all-to-all-done.1 = bf16[320,40,256]{2,1,0:T(8,128)(2,1)} async-done(((bf16[320,40,256]{2,1,0:T(8,128)(2,1)}), bf16[320,40,256]{2,1,0:T(8,128)(2,1)}, u32[]{:S(2)}, u32[]{:S(2)}) %all-to-all-start.1) | async-done | bytes 6553632 | tf_op jit(solution)/shard_map/all_to_all | solution.py:114
  520.2 45.7 %reduce-scatter.4.cloned.1.call-done = f32[768,4]{1,0:T(8,128)} async-done(((f32[6144,4]{1,0:T(8,128)}), f32[768,4]{1,0:T(8,128)}) %reduce-scatter.4.cloned.1.call-update) | async-done | bytes 12304
  (138 shorter events, 58.9 us)
Async XLA Ops:
  6.5 7.3 %copy-start = (bf16[4,6144]{1,0:T(4,128)(2,1)S(1)}, bf16[4,6144]{1,0:T(4,128)(2,1)}, u32[]{:S(2)}) copy-start(bf16[4,6144]{1,0:T(4,128)(2,1)} %param.9) | copy-start | bytes 147460
  12.6 1.2 copy-start.3
  12.7 1.2 copy-start.8
  13.8 0.9 copy-start.1
  36.3 16.7 %copy-start.10 = (f32[2,128]{1,0:T(2,128)S(1)}, f32[2,128]{1,0:T(2,128)}, u32[]{:S(2)}) copy-start(f32[2,128]{1,0:T(2,128)} %param.13) | copy-start | bytes 3076
  36.3 159.2 %all-to-all-start = ((bf16[320,40,256]{2,1,0:T(8,128)(2,1)}), bf16[320,40,256]{2,1,0:T(8,128)(2,1)}, u32[]{:S(2)}, u32[]{:S(2)}) async-start(bf16[320,40,256]{2,1,0:T(8,128)(2,1)} %broadcast_select_fusion), calls=%async_computation | async-start | bytes 13107200 | tf_op jit(solution)/shard_map/all_to_all | solution.py:104
  53.8 147.8 %copy-start.6 = (s32[256,1]{0,1:T(1,128)}, s32[256,1]{0,1:T(1,128)S(1)}, u32[]{:S(2)}) copy-start(s32[256,1]{0,1:T(1,128)S(1)} %compare_select_fusion.2) | copy-start | bytes 3076
  321.5 3.1 copy-start.7
  358.9 8.9 %copy-start.5 = (s32[64,5]{0,1:T(8,128)S(1)}, s32[64,5]{0,1:T(8,128)}, u32[]{:S(2)}) copy-start(s32[64,5]{0,1:T(8,128)} %get-tuple-element.109) | copy-start | bytes 3844
  358.9 9.2 %copy-start.2 = (f32[40,6144]{1,0:T(8,128)S(1)}, f32[40,6144]{1,0:T(8,128)}, u32[]{:S(2)}) copy-start(f32[40,6144]{1,0:T(8,128)} %copy-done.1) | copy-start | bytes 2949124
  358.9 152.9 %copy-start.4 = (s32[320]{0:T(512)S(1)}, s32[320]{0:T(512)}, u32[]{:S(2)}) copy-start(s32[320]{0:T(512)} %copy-done.3) | copy-start | bytes 3844
  358.9 152.9 %all-to-all-start.1 = ((bf16[320,40,256]{2,1,0:T(8,128)(2,1)}), bf16[320,40,256]{2,1,0:T(8,128)(2,1)}, u32[]{:S(2)}, u32[]{:S(2)}) async-start(bf16[320,40,256]{2,1,0:T(8,128)(2,1)} %scatter_fusion), calls=%async_computation.1 | async-start | bytes 13107200 | tf_op jit(solution)/shard_map/all_to_all | solution.py:114
  367.8 198.1 %reduce-scatter.4.cloned.1.call-start = ((), (), s32[]{:S(2)}) async-start(), calls=%async_computation.3 | async-start | bytes 3538944
  511.8 4.1 copy-start.9
Sparse Core Ops, SparseCore 0:
  520.3 45.5 reduce-scatter.3
where the time goes:
time: 578 us; the launch traced here: 574 us
  waiting for transfers between devices  331 us (57%)
  matrix products  105 us (18%)
  local copies, waits for them, and re-layouts  72.3 us (13%)
  other arithmetic  27.5 us (5%)
  starting transfers between devices  24.1 us (4%)
  between operations  14.3 us (2%)
    all_to_all x1, waiting for transfers between devices, shards(): lax.all_to_all(returned, 'col', split_axis=0, concat_axis=0, tiled=True)  143 us
    all_to_all x1, waiting for transfers between devices, shards(): lax.all_to_all(outgoing, 'col', split_axis=0, concat_axis=0, tiled=True)  142 us
    dot_general x8, matrix products, pair_results(): jnp.einsum('spq,smp->smq', taper, first_side, preferred_element_type=jnp....  48.4 us
    dot_general x8, matrix products, pair_results(): jnp.einsum('spq,smq->smp', taper, second_side, preferred_element_type=jnp...  48.2 us
    unnamed x2, waiting for transfers between devices  45.7 us
    scatter x1, local copies, waits for them, and re-layouts, shards(): jnp.zeros((owners * PEER_CAP, member_rows, BLOCK), jnp.bfloat16)  34.3 us
    all_to_all x1, starting transfers between devices, shards(): lax.all_to_all(outgoing, 'col', split_axis=0, concat_axis=0, tiled=True)  15.2 us
    gather x1, local copies, waits for them, and re-layouts, shards(): outgoing = jnp.take(weighted, chosen, axis=0)  14.1 us
  transfers between devices with their start and end apart: 3, of which 3 were waited for; matrix products, arithmetic and copies ran while one was open for 0% of the time, Pallas kernels for 0%

commit v1 on v0

v1 whole, which is shorter than its diff:
```python
import functools

import jax
import jax.numpy as jnp
import numpy as np
from jax import lax
from jax.experimental import pallas as pl
from jax.experimental.pallas import tpu as pltpu
from jax.sharding import PartitionSpec as P

MEMBERS = 80
LEVELS = 4
SIDE = 16
BLOCK = 256
SPACING_KM = 200.0
HALF_WIDTH = 250.0
XC = 8
LANES = 128


def gaspari_cohn(squared):
    scaled = jnp.sqrt(squared * (1.0 / (HALF_WIDTH * HALF_WIDTH)))
    near_part = (
        ((-0.25 * scaled + 0.5) * scaled + 0.625) * scaled - 5.0 / 3.0
    ) * scaled * scaled + 1.0
    bounded = jnp.maximum(scaled, 1.0)
    far_part = (
        ((((scaled * (1.0 / 12.0) - 0.5) * scaled + 0.625) * scaled + 5.0 / 3.0) * scaled - 5.0) * scaled
        + 4.0
        - (2.0 / 3.0) / bounded
    )
    return jnp.where(scaled <= 1.0, near_part, jnp.where(scaled <= 2.0, far_part, 0.0))


def lattice_offsets():
    giver = np.arange(SIDE)[:, None]
    lane = np.arange(BLOCK)[None, :]
    east = (giver - lane % SIDE) * SPACING_KM
    north = (SIDE // 2 - lane // SIDE) * SPACING_KM + 0 * giver
    return jnp.asarray(np.stack([east, north]).astype(np.float32))


def pair_kernel(blocks, table, row_count, shifts, live, offsets, weighted, ensemble, out, gram, total, work):
    total[...] = jnp.zeros_like(total)
    rows = row_count.shape[0]

    def scan_row(row, found):
        owner = row // 2
        count = live[owner]

        def scan_entry(k, found):
            word = table[row, k]
            slot = (row % 2) * (LANES // 2) + (word >> 17)

            @pl.when(slot < count)
            def _():
                work[found] = (word & 0xFFFF) | ((row * LANES + (word >> 16)) << 16)

            return found + (slot < count).astype(jnp.int32)

        return lax.fori_loop(0, row_count[row], scan_entry, found)

    found = lax.fori_loop(0, rows, scan_row, jnp.int32(0))

    lane = lax.broadcasted_iota(jnp.int32, (8, LANES), 1)

    def one(n, carry):
        word = work[n]
        receiver = word & 0xFF
        giver = (word >> 8) & 0xFF
        entry = word >> 16
        slot = entry // 2
        owner, place = slot // LANES, slot % LANES
        sign = (1 - 2 * (entry % 2)).astype(jnp.float32)
        east = sign * shifts[2 * owner, place]
        north = sign * shifts[2 * owner + 1, place]
        give = weighted[
            giver // blocks, :, pl.ds(pl.multiple_of((giver % blocks) * BLOCK, BLOCK), BLOCK)
        ]
        take = ensemble[
            receiver // blocks, :, pl.ds(pl.multiple_of((receiver % blocks) * BLOCK, BLOCK), BLOCK)
        ]
        gram[...] = lax.dot_general(
            give, take, (((0,), (0,)), ((), ())), preferred_element_type=jnp.float32
        )
        sums = [jnp.zeros((8, LANES), jnp.float32) for _ in range(2)]
        for half in range(2):
            rows_here = slice(8 * half, 8 * half + 8)
            parts = []
            for side in range(2):
                cols = slice(LANES * side, LANES * side + LANES)
                de = east + offsets[0, rows_here, cols]
                dn = north + offsets[1, rows_here, cols]
                tap = gaspari_cohn(de * de + dn * dn)
                parts.append(tap.astype(jnp.bfloat16).astype(jnp.float32))
            for k in range(8):
                turned = [pltpu.roll(p, 16 * k, 1) if k else p for p in parts]
                low = lane < 16 * k
                middle = jnp.where(low, turned[0], turned[1])
                first = jnp.where(low, 0.0, turned[0])
                last = jnp.where(low, turned[1], 0.0)
                at = 16 * k + 8 * half
                up = LANES + at
                sums[0] += middle * gram[at : at + 8, :LANES] + first * gram[up : up + 8, :LANES]
                sums[1] += last * gram[at : at + 8, LANES:] + middle * gram[up : up + 8, LANES:]
        total[receiver, :, :LANES] += sums[0]
        total[receiver, :, LANES:] += sums[1]
        return carry

    lax.fori_loop(0, found, one, 0)
    out[...] = jnp.sum(total[...], axis=1)


def entry_table(pair_home, pair_local, blocks, own_z, own_xc):
    home = pair_home.reshape(-1, 2)
    local = pair_local.reshape(-1, 2)
    other_home, other_local = home[:, ::-1], local[:, ::-1]
    mine = (home // XC == own_z) & (other_home % XC == own_xc)
    word = (home % XC) * blocks + local + (((other_home // XC) * blocks + other_local) << 8)
    mine = mine.reshape(-1, LANES)
    word = word.reshape(-1, LANES) + (jnp.arange(LANES)[None, :] << 16)
    before = np.triu(np.ones((LANES, LANES), np.float32), 1)
    rank = jnp.dot(
        mine.astype(jnp.bfloat16), jnp.asarray(before, jnp.bfloat16), preferred_element_type=jnp.float32
    ).astype(jnp.int32)
    rank = jnp.where(mine, rank, -1)
    table = jnp.sum(
        jnp.where(rank[:, :, None] == jnp.arange(LANES)[None, None, :], word[:, :, None], 0), axis=1
    )
    return table, jnp.sum(mine.astype(jnp.int32), axis=1)


def shards(ensemble, control, pair_home, pair_local, pair_count, pair_shift):
    member_rows, columns = ensemble.shape
    blocks = columns // BLOCK
    owners = lax.axis_size("col")
    own_index = lax.axis_index("col")
    own_level = (lax.axis_index("mem") * member_rows) // MEMBERS
    own_z, own_xc = own_index // XC, own_index % XC
    z_groups = [[z * XC + xc for z in range(owners // XC)] for xc in range(XC)]
    xc_groups = [[z * XC + xc for xc in range(XC)] for z in range(owners // XC)]

    shifts = lax.all_gather(pair_shift, "col").reshape(2 * owners, -1)
    live = lax.all_gather(pair_count, "col", tiled=True)
    own_control = lax.dynamic_index_in_dim(control, own_level, 0)
    weighted = (ensemble.astype(jnp.float32) * own_control.astype(jnp.float32)).astype(jnp.bfloat16)
    weighted = lax.all_gather(weighted, "col", axis_index_groups=z_groups)
    taking = lax.all_gather(ensemble, "col", axis_index_groups=xc_groups)
    table, row_count = entry_table(pair_home, pair_local, blocks, own_z, own_xc)

    smem = pl.BlockSpec(memory_space=pltpu.SMEM)
    vmem = pl.BlockSpec(memory_space=pltpu.VMEM)
    part = pl.pallas_call(
        functools.partial(pair_kernel, blocks),
        out_shape=jax.ShapeDtypeStruct((XC * blocks, BLOCK), jnp.float32),
        in_specs=[smem] * 4 + [vmem] * 3,
        out_specs=vmem,
        scratch_shapes=[
            pltpu.VMEM((BLOCK, BLOCK), jnp.float32),
            pltpu.VMEM((XC * blocks, 8, BLOCK), jnp.float32),
            pltpu.SMEM((pair_local.shape[0],), jnp.int32),
        ],
        compiler_params=pltpu.CompilerParams(vmem_limit_bytes=40 * 1024 * 1024),
    )(table, row_count, shifts, live, lattice_offsets(), weighted, taking)

    part = part.reshape(XC, columns)
    part = lax.all_to_all(part, "col", 0, 0, axis_index_groups=xc_groups, tiled=True)
    part = jnp.sum(part, axis=0).reshape(lax.axis_size("mem"), -1)
    part = lax.all_to_all(part, "mem", 0, 0, tiled=True)
    return jnp.sum(part.reshape(LEVELS, -1, part.shape[1]), axis=1) / (MEMBERS - 1.0)


def solution(mesh):
    return jax.shard_map(
        shards,
        mesh=mesh,
        in_specs=(P("mem", "col"), P(None, "col"), P(), P(), P("col"), P(None, "col")),
        out_specs=P(None, ("col", "mem")),
        check_vma=False,
    )
```

time: 578 us -> 285 us (0.49)
  the two profiles are of different devices: /device:TPU:1 before, /device:TPU:128 now
where the time goes in v1:
time: 285 us; the launch traced here: 280 us
  blocking collectives  93.8 us (33%)
  local copies, waits for them, and re-layouts  93.3 us (33%)
  Pallas kernels  52.9 us (19%)
  other arithmetic  24.9 us (9%)
  between operations  14.2 us (5%)
    rev x2, local copies, waits for them, and re-layouts, entry_table(): other_home, other_local = (home[:, ::-1], local[:, ::-1])  68 us
    pallas_call x1, Pallas kernels, shards(): pl.pallas_call(functools.partial(pair_kernel, blocks), out_shape=jax.Shap...  52.9 us
    all_gather x1, blocking collectives, shards(): shifts = lax.all_gather(pair_shift, 'col').reshape(2 * owners, -1)  40.9 us
    unnamed x1, blocking collectives  23.3 us
    all_to_all x1, blocking collectives, shards(): lax.all_to_all(part, 'col', 0, 0, axis_index_groups=xc_groups, tiled=True)  14.9 us
    all_to_all x1, blocking collectives, shards(): part = lax.all_to_all(part, 'mem', 0, 0, tiled=True)  14.7 us
    reduce_sum x2, other arithmetic, entry_table(): return (table, jnp.sum(mine.astype(jnp.int32), axis=1))  14.1 us
    unnamed x16, local copies, waits for them, and re-layouts  6.77 us
  transfers between devices with their start and end apart: 2, of which 0 were waited for; matrix products, arithmetic and copies ran while one was open for 39% of the time, Pallas kernels for 0%

profile of v1, /device:TPU:128, one launch (start us, length us, event | category | flops | bytes accessed | tf_op | source)
XLA Modules:
  0.0 280.1 jit_solution(15174083226945311041)
XLA Ops:
  6.5 0.8 dynamic-slice_convert_fusion
  7.4 1.9 multiply_convert_fusion
  9.3 0.7 all-gather.9.cloned.1.call-update
  10.1 0.5 broadcast.48
  10.6 1.6 reduce.7
  12.2 5.5 %reshape.51 = s32[8192,2]{1,0:T(8,128)} reshape(s32[16384]{0:T(1024)S(1)} %reduce.7) | data formatting | bytes 131072 | tf_op jit(solution)/shard_map/reshape | solution.py:115
  17.7 34.0 %rev.6 = s32[8192,2]{1,0:T(8,128)} reverse(s32[8192,2]{1,0:T(8,128)} %reshape.51), dimensions={1} | reverse | bytes 131072 | tf_op jit(solution)/shard_map/rev | solution.py:117
  51.7 5.5 %reshape.53 = s32[8192,2]{1,0:T(8,128)} reshape(s32[16384]{0:T(1024)S(1)} %copy-done.3) | data formatting | bytes 131072 | tf_op jit(solution)/shard_map/reshape | solution.py:116
  57.3 34.0 %rev.7 = s32[8192,2]{1,0:T(8,128)} reverse(s32[8192,2]{1,0:T(8,128)} %reshape.53), dimensions={1} | reverse | bytes 131072 | tf_op jit(solution)/shard_map/rev | solution.py:117
  91.3 14.0 %convert_reduce_fusion = (s32[8192]{0:T(1024)S(1)}, pred[8192,2]{1,0:T(32,128)(4,1)S(1)}, s32[8192,2]{1,0:T(8,128)}) fusion(s32[]{:T(128)S(6)} %select_n.47, s32[8192,2]{1,0:T(8,128)} %rev.6, s32[]{:T(128)S(6)} %select_n.45, s32[8192,2]{1,0:T(8,128)} %reshape.51, s32[8192,2]{1,0:T(8,128)} %rev.7, s32[8192,2]{1,0:T(8,128)} %reshape.53), kind=kLoop, calls=%fused_computation.20 | loop fusion | flops 794624 | bytes 376840 | tf_op jit(solution)/shard_map/reduce_sum | solution.py:130
  105.2 4.0 %reshape.54 = s32[128,128]{1,0:T(8,128)S(1)} reshape(s32[8192,2]{1,0:T(8,128)} %get-tuple-element.7) | data formatting | bytes 131072 | tf_op jit(solution)/shard_map/reshape | solution.py:121
  109.3 3.1 %reshape.52 = pred[128,128]{1,0:T(32,128)(4,1)S(1)} reshape(pred[8192,2]{1,0:T(32,128)(4,1)S(1)} %get-tuple-element.6) | data formatting | bytes 32768 | tf_op jit(solution)/shard_map/reshape | solution.py:120
  113.3 1.3 dynamic-slice
  114.5 0.8 dynamic-update-slice
  115.3 23.3 %all-reduce.live = s32[64]{0:T(128)S(1)} all-reduce(s32[64]{0:T(128)S(1)} %dynamic-update-slice), channel_id=1, replica_groups=mesh['col'=64,'mem'=8] {'col'}, use_global_device_ids=true, to_apply=%add | all-reduce | flops 64 | bytes 512
  138.6 40.9 %all-gather.3 = f32[64,2,128]{2,1,0:T(2,128)S(1)} all-gather(f32[1,2,128]{2,1,0:T(2,128)S(1)} %bitcast.15), channel_id=2, replica_groups=mesh['col'=64,'mem'=8] {'col'}, dimensions={0}, use_global_device_ids=true | all-gather | bytes 66560 | tf_op jit(solution)/shard_map/all_gather | solution.py:143
  179.7 5.6 %select_reduce_fusion.table = s32[128,128]{1,0:T(8,128)S(1)} fusion(s32[128,128]{1,0:T(8,128)S(1)} %broadcast_add_fusion, s32[128,128]{1,0:T(8,128)S(1)} %fusion.13), kind=kLoop, calls=%fused_computation | loop fusion | flops 6275072 | bytes 196608 | tf_op jit(solution)/shard_map/reduce_sum | solution.py:127
  185.4 2.1 copy-done
  187.5 2.1 copy-done.1
  189.6 52.9 %shard_map.82 = f32[192,256]{1,0:T(8,128)S(1)} custom-call(s32[128,128]{1,0:T(8,128)S(1)} %select_reduce_fusion.table, s32[128]{0:T(128)S(1)} %reduce_sum.46.row_count, f32[128,128]{1,0:T(8,128)S(1)} %bitcast.12, s32[64]{0:T(128)S(1)} %all-reduce.live, f32[2,16,256]{2,1,0:T(8,128)S(1)} %copy-done.2, bf16[8,40,6144]{2,1,0:T(8,128)(2,1)S(1)} %bitcast.10, ...), custom_call_target="tpu_custom_call" | custom-call | tf_op jit(solution)/shard_map/pallas_call | solution.py:153
  242.5 0.2 all_to_all.16
  242.7 14.9 %all_to_all.19 = f32[8,1,6144]{2,1,0:T(1,128)S(1)} all-to-all(f32[8,1,6144]{2,1,0:T(1,128)S(1)} %all_to_all.16), channel_id=1, replica_groups={{0,8,16,24,32,40,48,56},{64,72,80,88,96,104,112,120},{128,136,144,152,1..., dimensions={0} | all-to-all | bytes 393216 | tf_op jit(solution)/shard_map/all_to_all | solution.py:167
  257.8 14.7 %all_to_all.20 = f32[8,1,768]{2,1,0:T(1,128)S(1)} all-to-all(f32[8,1,768]{2,1,0:T(1,128)S(1)} %bitcast.13), channel_id=1, replica_groups=mesh['col'=64,'mem'=8] {'mem'}, dimensions={0} | all-to-all | bytes 49152 | tf_op jit(solution)/shard_map/all_to_all | solution.py:169
  272.6 0.6 broadcast_multiply_fusion
  (25 shorter events, 0.7 us)
Async XLA Ops:
  6.5 178.8 %all-gather.7.cloned.1.call-start = ((), (), s32[]{:S(2)}) async-start(), calls=%async_computation.2 | async-start | bytes 4423680 | tf_op jit(solution)/shard_map/all_gather | solution.py:147
  9.3 176.1 %all-gather.9.cloned.1.call-start = ((), (), s32[]{:S(2)}) async-start(), calls=%async_computation.3 | async-start | bytes 4423680 | tf_op jit(solution)/shard_map/all_gather | solution.py:148
  17.7 34.0 %copy-start.3 = (s32[16384]{0:T(1024)S(1)}, s32[16384]{0:T(1024)}, u32[]{:S(2)}) copy-start(s32[16384]{0:T(1024)} %param.11) | copy-start | bytes 196612
  105.2 33.4 %copy-start.5 = (f32[2,128]{1,0:T(2,128)S(1)}, f32[2,128]{1,0:T(2,128)}, u32[]{:S(2)}) copy-start(f32[2,128]{1,0:T(2,128)} %param.13) | copy-start | bytes 3076
  105.2 74.3 %copy-start.4 = (bf16[128,128]{1,0:T(8,128)(2,1)S(1)}, bf16[128,128]{1,0:T(8,128)(2,1)}, u32[]{:S(2)}) copy-start(bf16[128,128]{1,0:T(8,128)(2,1)} %constant.93.clone) | copy-start | bytes 98308
  105.2 80.2 %copy-start.2 = (f32[2,16,256]{2,1,0:T(8,128)S(1)}, f32[2,16,256]{2,1,0:T(8,128)}, u32[]{:S(2)}) copy-start(f32[2,16,256]{2,1,0:T(8,128)} %constant.94.clone.offsets) | copy-start | bytes 98308
  185.4 2.1 copy-start
  187.5 2.1 copy-start.1
Sparse Core Ops, SparseCore 0:
  9.4 57.0 all-gather.6
  68.6 36.3 all-gather.8

commit v2 on v1

v2 whole, which is shorter than its diff:
```python
import functools

import jax
import jax.numpy as jnp
import numpy as np
from jax import lax
from jax.experimental import pallas as pl
from jax.experimental.pallas import tpu as pltpu
from jax.sharding import PartitionSpec as P

MEMBERS = 80
LEVELS = 4
SIDE = 16
BLOCK = 256
SPACING_KM = 200.0
HALF_WIDTH = 250.0
XC = 8
Z = 8
X = 4
GROUP = 4
MESH_ID = pl.DeviceIdType.MESH
LANES = 128


def gaspari_cohn(squared):
    scaled = jnp.sqrt(squared * (1.0 / (HALF_WIDTH * HALF_WIDTH)))
    near_part = (
        ((-0.25 * scaled + 0.5) * scaled + 0.625) * scaled - 5.0 / 3.0
    ) * scaled * scaled + 1.0
    bounded = jnp.maximum(scaled, 1.0)
    far_part = (
        ((((scaled * (1.0 / 12.0) - 0.5) * scaled + 0.625) * scaled + 5.0 / 3.0) * scaled - 5.0) * scaled
        + 4.0
        - (2.0 / 3.0) / bounded
    )
    return jnp.where(scaled <= 1.0, near_part, jnp.where(scaled <= 2.0, far_part, 0.0))


def lattice_offsets():
    giver = np.arange(SIDE)[:, None]
    lane = np.arange(BLOCK)[None, :]
    east = (giver - lane % SIDE) * SPACING_KM
    north = (SIDE // 2 - lane // SIDE) * SPACING_KM + 0 * giver
    return jnp.asarray(np.stack([east, north]).astype(np.float32))


def place():
    col = lax.axis_index("col")
    return col, col // XC, (col % XC) // 2, col % 2


def row_peer(z, x, core, slot):
    return {"col": z * XC + lax.rem(x + slot // 2, X) * 2 + lax.rem(core + slot % 2, 2)}


def column_peer(col, z, step):
    return {"col": col + (lax.rem(z + step, Z) - z) * XC}


def mirrored(slot):
    return (X - slot // 2) % X * 2 + slot % 2


def enter(peers):
    barrier = pltpu.get_barrier_semaphore()
    for peer in peers:
        pl.semaphore_signal(barrier, inc=1, device_id=peer, device_id_type=MESH_ID)
    pl.semaphore_wait(barrier, len(peers))


def turn(a, shift):
    return pltpu.roll(a, shift % a.shape[1], 1)


def make_table(home, local, count, blocks, z, x, core):
    lanes = home.shape[1]
    lane = lax.broadcasted_iota(jnp.int32, home.shape, 1)
    even = (lane & 1) == 0
    other_home = jnp.where(even, turn(home, -1), turn(home, 1))
    other_local = jnp.where(even, turn(local, -1), turn(local, 1))
    mine = ((home >> 3) == z) & ((other_home & 7) == x * 2 + core) & ((lane >> 1) < count)
    slot = ((((home >> 1) & 3) - x) & 3) * 2 + ((home ^ core) & 1)
    turned = ((other_home >> 3) - z) & 7
    word = (slot * blocks + local) | ((turned * blocks + other_local) << 8) | (lane << 16)
    rank = mine.astype(jnp.int32)
    step = 1
    while step < lanes:
        rank = rank + jnp.where(lane >= step, turn(rank, step), 0)
        step *= 2
    found = rank[:, lanes - LANES :]
    found = jnp.max(found, axis=1, keepdims=True)
    value = jnp.where(mine, word, -1)
    move = jnp.where(mine, lane - rank + 1, 0)
    step = 1
    while step < lanes:
        next_value, next_move = turn(value, -step), turn(move, -step)
        arrives, leaves = (next_move & step) != 0, (move & step) != 0
        value = jnp.where(arrives, next_value, jnp.where(leaves, -1, value))
        move = jnp.where(arrives, next_move, jnp.where(leaves, 0, move))
        step *= 2
    return value, jnp.broadcast_to(found, (home.shape[0], LANES))


def gather_kernel(
    blocks, ensemble, control, small, home, local,
    weighted, taking, table, found, east, north,
    seen, z_send, z_recv, x_send, x_recv, core_send, core_recv, row_send, row_recv, col_send, col_recv,
):
    col, z, x, core = place()
    member_rows, columns = ensemble.shape
    half = columns // 2
    level = (lax.axis_index("mem") * member_rows) // MEMBERS
    scale = jnp.zeros((1, columns), jnp.float32)
    for l in range(LEVELS):
        scale = jnp.where(level == l, control[l : l + 1, :].astype(jnp.float32), scale)
    weighted[0] = (ensemble[...].astype(jnp.float32) * scale).astype(jnp.bfloat16)
    taking[0] = ensemble[...]
    seen[pl.ds(pl.multiple_of(col * 8, 8), 8), :] = small[...]

    enter([row_peer(z, x, core, s) for s in range(1, XC)] + [column_peer(col, z, s) for s in range(1, Z)])

    sent = []

    def send(source, target, send_sem, recv_sem, peer):
        copy = pltpu.make_async_remote_copy(
            src_ref=source, dst_ref=target, send_sem=send_sem, recv_sem=recv_sem,
            device_id=peer, device_id_type=MESH_ID,
        )
        copy.start()
        sent.append(copy)
        return copy

    def part(ref, slot, c):
        return ref.at[slot, :, pl.ds(c * half, half)]

    def send_z(way, step, c):
        sign = 1 if way == 0 else -1
        return send(
            part(weighted, (-sign * step) % Z, c), part(weighted, (-sign * (step + 1)) % Z, c),
            z_send.at[way, step, c], z_recv.at[way, step, c], column_peer(col, z, sign % Z),
        )

    def send_x(way, step, c):
        sign = 1 if way == 0 else -1
        return send(
            part(taking, (-sign * step) % X * 2, c), part(taking, (-sign * (step + 1)) % X * 2, c),
            x_send.at[way, step, c], x_recv.at[way, step, c], row_peer(z, x, core, sign % X * 2),
        )

    def send_core(turned, c):
        return send(
            part(taking, turned * 2, c), part(taking, turned * 2 + 1, c),
            core_send.at[turned, c], core_recv.at[turned, c], row_peer(z, x, core, 1),
        )

    row_copies = []
    own_rows = seen.at[pl.ds(pl.multiple_of(col * 8, 8), 8), :]
    for s in range(1, XC):
        row_copies.append(send(own_rows, own_rows, row_send.at[s], row_recv.at[s], row_peer(z, x, core, s)))
    zs, xs, cores = {}, {}, []
    for c in range(2):
        for way in range(2):
            zs[way, 0, c] = send_z(way, 0, c)
            xs[way, 0, c] = send_x(way, 0, c)
    for c in range(2):
        cores.append(send_core(0, c))
    for copy in row_copies:
        copy.wait_recv()
    col_copies = []
    z_rows = seen.at[pl.ds(pl.multiple_of(z * 64, 64), 64), :]
    for s in range(1, Z):
        col_copies.append(send(z_rows, z_rows, col_send.at[s], col_recv.at[s], column_peer(col, z, s)))

    for step in range(4):
        for c in range(2):
            for way in range(2):
                if step < 3 or c == way:
                    zs[way, step, c].wait_recv()
                    if step < 2 or (step == 2 and c == way):
                        zs[way, step + 1, c] = send_z(way, step + 1, c)
            for way in range(2):
                turned = (-(1 if way == 0 else -1) * (step + 1)) % X
                if step == 0 or (step == 1 and c == way):
                    xs[way, step, c].wait_recv()
                    if step == 0 and c == way:
                        xs[way, 1, c] = send_x(way, 1, c)
                    cores.append(send_core(turned, c))
        if step == 0:
            for copy in col_copies:
                copy.wait_recv()
            owners = seen.shape[0] // 8
            count = seen[pl.ds(2, owners, stride=8), :]
            count = jnp.concatenate([count, count], axis=1).astype(jnp.int32)
            table[...], found[...] = make_table(home[...], local[...], count, blocks, z, x, core)
            east[...] = seen[pl.ds(0, owners, stride=8), :]
            north[...] = seen[pl.ds(1, owners, stride=8), :]
    for copy in cores:
        copy.wait_recv()
    for copy in sent:
        copy.wait_send()


def pair_kernel(blocks, table, found, east, north, offsets, weighted, ensemble, out, total, work, *grams):
    total[...] = jnp.zeros_like(total)

    def scan_row(row, base):
        def scan_entry(k, base):
            word = table[row, k]
            work[base] = (word & 0xFFFF) | ((row * 2 * LANES + (word >> 16)) << 16)
            return base + 1

        return lax.fori_loop(0, found[row, 0], scan_entry, base)

    amount = lax.fori_loop(0, table.shape[0], scan_row, jnp.int32(0))
    for g in range(GROUP - 1):
        work[amount + g] = -1

    lane = lax.broadcasted_iota(jnp.int32, (8, LANES), 1)

    def one(word, gram):
        live = word >= 0
        word = jnp.where(live, word, 0)
        receiver = word & 0xFF
        giver = (word >> 8) & 0xFF
        entry = word >> 16
        owner, place_in = entry >> 8, (entry & 0xFF) >> 1
        sign = (1 - 2 * (entry & 1)).astype(jnp.float32)
        shift_e = jnp.where(live, sign * east[owner, place_in], 1e5)
        shift_n = sign * north[owner, place_in]
        give = weighted[
            giver // blocks, :, pl.ds(pl.multiple_of((giver % blocks) * BLOCK, BLOCK), BLOCK)
        ]
        take = ensemble[
            receiver // blocks, :, pl.ds(pl.multiple_of((receiver % blocks) * BLOCK, BLOCK), BLOCK)
        ]
        gram[...] = lax.dot_general(
            give, take, (((0,), (0,)), ((), ())), preferred_element_type=jnp.float32
        )
        sums = [jnp.zeros((8, LANES), jnp.float32) for _ in range(2)]
        for half in range(2):
            rows_here = slice(8 * half, 8 * half + 8)
            parts = []
            for side in range(2):
                cols = slice(LANES * side, LANES * side + LANES)
                de = shift_e + offsets[0, rows_here, cols]
                dn = shift_n + offsets[1, rows_here, cols]
                tap = gaspari_cohn(de * de + dn * dn)
                parts.append(tap.astype(jnp.bfloat16).astype(jnp.float32))
            for k in range(8):
                turned = [pltpu.roll(p, 16 * k, 1) if k else p for p in parts]
                low = lane < 16 * k
                middle = jnp.where(low, turned[0], turned[1])
                first = jnp.where(low, 0.0, turned[0])
                last = jnp.where(low, turned[1], 0.0)
                at = 16 * k + 8 * half
                up = LANES + at
                sums[0] += middle * gram[at : at + 8, :LANES] + first * gram[up : up + 8, :LANES]
                sums[1] += last * gram[at : at + 8, LANES:] + middle * gram[up : up + 8, LANES:]
        return receiver, sums

    def some(n, carry):
        done = [one(work[n * GROUP + g], grams[g]) for g in range(GROUP)]
        for receiver, sums in done:
            total[receiver, :, :LANES] += sums[0]
            total[receiver, :, LANES:] += sums[1]
        return carry

    lax.fori_loop(0, (amount + GROUP - 1) // GROUP, some, 0)
    out[...] = jnp.sum(total[...], axis=1).reshape(out.shape)


def sum_kernel(part, out, rows_in, mine, pieces, row_send, row_recv, mem_send, mem_recv):
    _, z, x, core = place()
    mem = lax.axis_index("mem")
    mems = mine.shape[0]

    def mem_peer(step):
        return {"mem": lax.rem(mem + step, mems)}

    enter([row_peer(z, x, core, s) for s in range(1, XC)] + [mem_peer(s) for s in range(1, mems)])
    copies = []
    for s in range(1, XC):
        copy = pltpu.make_async_remote_copy(
            src_ref=part.at[s], dst_ref=rows_in.at[mirrored(s)],
            send_sem=row_send.at[s], recv_sem=row_recv.at[mirrored(s)],
            device_id=row_peer(z, x, core, s), device_id_type=MESH_ID,
        )
        copy.start()
        copies.append(copy)
    summed = part[0]
    for s in range(1, XC):
        copies[s - 1].wait()
    for s in range(1, XC):
        summed = summed + rows_in[s]
    each = summed.shape[0] // mems
    for m in range(mems):
        mine[m, :each, :] = summed[m * each : (m + 1) * each, :]
        mine[m, each:, :] = jnp.zeros((mine.shape[1] - each, BLOCK), jnp.float32)
    pieces[mem] = mine[mem]
    copies = []
    for s in range(1, mems):
        copy = pltpu.make_async_remote_copy(
            src_ref=mine.at[lax.rem(mem + s, mems)], dst_ref=pieces.at[mem],
            send_sem=mem_send.at[s], recv_sem=mem_recv.at[s],
            device_id=mem_peer(s), device_id_type=MESH_ID,
        )
        copy.start()
        copies.append(copy)
    for copy in copies:
        copy.wait()
    for l in range(LEVELS):
        first = l * (mems // LEVELS)
        both = pieces[first]
        for m in range(first + 1, first + mems // LEVELS):
            both = both + pieces[m]
        both = both / (MEMBERS - 1.0)
        for i in range(each):
            out[l : l + 1, i * BLOCK : (i + 1) * BLOCK] = both[i : i + 1, :]


def shards(ensemble, control, pair_home, pair_local, pair_count, pair_shift):
    member_rows, columns = ensemble.shape
    blocks = columns // BLOCK
    owners = lax.axis_size("col")
    mems = lax.axis_size("mem")
    small = jnp.concatenate(
        [pair_shift, jnp.broadcast_to(pair_count.astype(jnp.float32)[:, None], (1, LANES)), jnp.zeros((5, LANES), jnp.float32)]
    )
    home = pair_home.reshape(owners, -1)
    local = pair_local.reshape(owners, -1)
    smem = pl.BlockSpec(memory_space=pltpu.SMEM)
    vmem = pl.BlockSpec(memory_space=pltpu.VMEM)
    dma = pltpu.SemaphoreType.DMA

    weighted, taking, table, found, east, north = pl.pallas_call(
        functools.partial(gather_kernel, blocks),
        out_shape=(
            jax.ShapeDtypeStruct((Z, member_rows, columns), jnp.bfloat16),
            jax.ShapeDtypeStruct((XC, member_rows, columns), jnp.bfloat16),
            jax.ShapeDtypeStruct(home.shape, jnp.int32),
            jax.ShapeDtypeStruct((owners, LANES), jnp.int32),
            jax.ShapeDtypeStruct((owners, LANES), jnp.float32),
            jax.ShapeDtypeStruct((owners, LANES), jnp.float32),
        ),
        in_specs=[vmem] * 5,
        out_specs=[vmem] * 6,
        scratch_shapes=[
            pltpu.VMEM((owners * 8, LANES), jnp.float32),
            dma((2, 4, 2)), dma((2, 4, 2)), dma((2, 2, 2)), dma((2, 2, 2)), dma((X, 2)), dma((X, 2)),
            dma((XC,)), dma((XC,)), dma((Z,)), dma((Z,)),
        ],
        compiler_params=pltpu.CompilerParams(
            collective_id=0, has_side_effects=True, vmem_limit_bytes=40 * 1024 * 1024
        ),
    )(ensemble, control, small, home, local)

    part = pl.pallas_call(
        functools.partial(pair_kernel, blocks),
        out_shape=jax.ShapeDtypeStruct((XC, blocks, BLOCK), jnp.float32),
        in_specs=[smem] * 4 + [vmem] * 3,
        out_specs=vmem,
        scratch_shapes=[
            pltpu.VMEM((XC * blocks, 8, BLOCK), jnp.float32),
            pltpu.SMEM((pair_local.shape[0] + GROUP,), jnp.int32),
        ] + [pltpu.VMEM((BLOCK, BLOCK), jnp.float32)] * GROUP,
        compiler_params=pltpu.CompilerParams(vmem_limit_bytes=40 * 1024 * 1024),
    )(table, found, east, north, lattice_offsets(), weighted, taking)

    return pl.pallas_call(
        sum_kernel,
        out_shape=jax.ShapeDtypeStruct((LEVELS, columns // mems), jnp.float32),
        in_specs=[vmem],
        out_specs=vmem,
        scratch_shapes=[
            pltpu.VMEM((XC, blocks, BLOCK), jnp.float32),
            pltpu.VMEM((mems, 8, BLOCK), jnp.float32),
            pltpu.VMEM((mems, 8, BLOCK), jnp.float32),
            dma((XC,)), dma((XC,)), dma((mems,)), dma((mems,)),
        ],
        compiler_params=pltpu.CompilerParams(
            collective_id=1, has_side_effects=True, vmem_limit_bytes=8 * 1024 * 1024
        ),
    )(part)


def solution(mesh):
    return jax.shard_map(
        shards,
        mesh=mesh,
        in_specs=(P("mem", "col"), P(None, "col"), P(), P(), P("col"), P(None, "col")),
        out_specs=P(None, ("col", "mem")),
        check_vma=False,
    )
```

time: 285 us -> 103 us (0.36)
  the two profiles are of different devices: /device:TPU:128 before, /device:TPU:1 now
where the time goes in v2:
time: 103 us; the launch traced here: 102 us
  Pallas kernels  94.6 us (92%)
  local copies, waits for them, and re-layouts  4.72 us (5%)
  other arithmetic  2.39 us (2%)
    pallas_call x1, Pallas kernels, shards(): pl.pallas_call(functools.partial(gather_kernel, blocks), out_shape=(jax.S...  58 us
    pallas_call x1, Pallas kernels, shards(): pl.pallas_call(functools.partial(pair_kernel, blocks), out_shape=jax.Shap...  22.4 us
    pallas_call x1, Pallas kernels, shards(): pl.pallas_call(sum_kernel, out_shape=jax.ShapeDtypeStruct((LEVELS, column...  14.2 us
    unnamed x8, local copies, waits for them, and re-layouts  3.69 us

profile of v2, /device:TPU:1, one launch (start us, length us, event | category | flops | bytes accessed | tf_op | source)
XLA Modules:
  0.0 102.4 jit_solution(730885653358593805)
XLA Ops:
  0.7 0.1 pad.1.clone
  0.7 0.1 pad.2.clone
  0.8 0.8 maximum_maximum_fusion.small
  1.6 0.5 broadcast.8
  2.1 1.6 %reduce.3 = s32[16384]{0:T(1024)S(1)} reduce(s32[16384,1]{0,1:T(1,128)} %param.9, s32[]{:T(128)} %broadcast.8), dimensions={1}, to_apply=%param.9.reduce_sub_computation.3 | reduce | bytes 131076 | tf_op args[2]
  3.7 0.9 reshape.10.local
  4.6 0.0 copy-start
  4.6 1.0 copy-done
  5.6 0.0 copy-start.1
  5.6 0.8 copy-done.1
  6.4 58.0 %shard_map.73 = (bf16[8,40,6144]{2,1,0:T(8,128)(2,1)S(1)}, bf16[8,40,6144]{2,1,0:T(8,128)(2,1)S(1)}, s32[64,256]{1,0:T(8,128)S(1)}, s32[64,128]{1,0:T(8,128)S(1)...) custom-call(bf16[40,6144]{1,0:T(8,128)(2,1)S(1)} %copy-done, bf16[4,6144]{1,0:T(4,128)(2,1)S(1)} %copy-done.1, ...), custom_call_target="tpu_custom_call" | custom-call | tf_op jit(solution)/shard_map/pallas_call | solution.py:335
  64.4 0.0 copy-start.2
  64.4 0.7 copy-done.2
  65.2 22.4 %shard_map.74.part = f32[8,24,256]{2,1,0:T(8,128)S(1)} custom-call(s32[64,256]{1,0:T(8,128)S(1)} %get-tuple-element.11.table, s32[64,128]{1,0:T(8,128)S(1)} %get-tuple-element.12.found, f32[64,128]{1,0:T(8,128)S(1)} %get-tuple-element.13.east, f32[64,128]{1,0:T(8,128)S(1)} %get-tuple-element.14.north, f32[2,16,256]{2,1,0:T(8,128)S(1)} %copy-done.2, ...), custom_call_target="tpu_custom_call" | custom-call | tf_op jit(solution)/shard_map/pallas_call | solution.py:357
  87.6 14.2 %shard_map.75 = f32[4,768]{1,0:T(4,128)S(1)} custom-call(f32[8,24,256]{2,1,0:T(8,128)S(1)} %shard_map.74.part), custom_call_target="tpu_custom_call" | custom-call | tf_op jit(solution)/shard_map/pallas_call | solution.py:369
  101.8 0.6 copy.10
  (2 shorter events, 0.0 us)
Async XLA Ops:
  4.6 1.0 %copy-start = (bf16[40,6144]{1,0:T(8,128)(2,1)S(1)}, bf16[40,6144]{1,0:T(8,128)(2,1)}, u32[]{:S(2)}) copy-start(bf16[40,6144]{1,0:T(8,128)(2,1)} %ensemble.1) | copy-start | bytes 1474564
  5.6 0.8 copy-start.1
  64.4 0.8 copy-start.2

commit v3 on v2

v3 whole, which is shorter than its diff:
```python
import functools

import jax
import jax.numpy as jnp
import numpy as np
from jax import lax
from jax.experimental import pallas as pl
from jax.experimental.pallas import tpu as pltpu
from jax.sharding import PartitionSpec as P

MEMBERS = 80
LEVELS = 4
SIDE = 16
BLOCK = 256
SPACING_KM = 200.0
HALF_WIDTH = 250.0
XC = 8
CAP = 32
ROW_CAP = 16
STRIPE = 2 * CAP
Z = 8
X = 4
GROUP = 4
MESH_ID = pl.DeviceIdType.MESH
LANES = 128


def gaspari_cohn(squared):
    scaled = jnp.sqrt(squared * (1.0 / (HALF_WIDTH * HALF_WIDTH)))
    near_part = (
        ((-0.25 * scaled + 0.5) * scaled + 0.625) * scaled - 5.0 / 3.0
    ) * scaled * scaled + 1.0
    bounded = jnp.maximum(scaled, 1.0)
    far_part = (
        ((((scaled * (1.0 / 12.0) - 0.5) * scaled + 0.625) * scaled + 5.0 / 3.0) * scaled - 5.0) * scaled
        + 4.0
        - (2.0 / 3.0) / bounded
    )
    return jnp.where(scaled <= 1.0, near_part, jnp.where(scaled <= 2.0, far_part, 0.0))


def lattice_offsets():
    giver = np.arange(SIDE)[:, None]
    lane = np.arange(BLOCK)[None, :]
    east = (giver - lane % SIDE) * SPACING_KM
    north = (SIDE // 2 - lane // SIDE) * SPACING_KM + 0 * giver
    return jnp.asarray(np.stack([east, north]).astype(np.float32))


def place():
    col = lax.axis_index("col")
    return col, col // XC, (col % XC) // 2, col % 2


def row_peer(z, x, core, slot):
    return {"col": z * XC + lax.rem(x + slot // 2, X) * 2 + lax.rem(core + slot % 2, 2)}


def column_peer(col, z, step):
    return {"col": col + (lax.rem(z + step, Z) - z) * XC}


def mirrored(slot):
    return (X - slot // 2) % X * 2 + slot % 2


def enter(peers):
    barrier = pltpu.get_barrier_semaphore()
    for peer in peers:
        pl.semaphore_signal(barrier, inc=1, device_id=peer, device_id_type=MESH_ID)
    pl.semaphore_wait(barrier, len(peers))


def turn(a, shift):
    return pltpu.roll(a, shift % a.shape[1], 1)


def own_entries(home, local, count, z, x, core):
    lane = lax.broadcasted_iota(jnp.int32, home.shape, 1)
    even = (lane & 1) == 0
    other_home = jnp.where(even, turn(home, -1), turn(home, 1))
    other_local = jnp.where(even, turn(local, -1), turn(local, 1))
    mine = ((home >> 3) == z) & ((other_home & 7) == x * 2 + core) & ((lane >> 1) < count)
    slot = ((((home >> 1) & 3) - x) & 3) * 2 + ((home ^ core) & 1)
    turned = ((other_home >> 3) - z) & 7
    return mine, slot, other_local, turned


def row_rank(mine):
    rank = mine.astype(jnp.int32)
    lane = lax.broadcasted_iota(jnp.int32, rank.shape, 1)
    step = 1
    while step < rank.shape[1]:
        rank = rank + jnp.where(lane >= step, turn(rank, step), 0)
        step *= 2
    return rank - 1


def pack_rows(mine, rank, arrays):
    lane = lax.broadcasted_iota(jnp.int32, rank.shape, 1)
    move = jnp.where(mine, lane - rank, 0)
    arrays = [jnp.where(mine, a, 0) for a in arrays]
    step = 1
    while step < rank.shape[1]:
        next_move = turn(move, -step)
        arrives, leaves = (next_move & step) != 0, (move & step) != 0
        arrays = [jnp.where(arrives, turn(a, -step), jnp.where(leaves, 0, a)) for a in arrays]
        move = jnp.where(arrives, next_move, jnp.where(leaves, 0, move))
        step *= 2
    return arrays


def group_rank(mine, turned):
    rows, lanes = mine.shape
    line = lax.broadcasted_iota(jnp.int32, (rows, lanes), 0)
    lane = lax.broadcasted_iota(jnp.int32, (rows, lanes), 1)
    rank = jnp.zeros((rows, lanes), jnp.int32)
    for t in range(0, Z, 2):
        low, high = mine & (turned == t), mine & (turned == t + 1)
        upto = low.astype(jnp.int32) + (high.astype(jnp.int32) << 16)
        step = 1
        while step < lanes:
            upto = upto + jnp.where(lane >= step, turn(upto, step), 0)
            step *= 2
        whole = jnp.broadcast_to(upto[:, lanes - 1 :], (rows, lanes))
        above = whole
        step = 1
        while step < rows:
            above = above + jnp.where(line >= step, pltpu.roll(above, step, 0), 0)
            step *= 2
        upto = upto + above - whole
        rank = jnp.where(low, (upto & 0xFFFF) - 1, jnp.where(high, (upto >> 16) - 1, rank))
    return rank


def make_lists(mine, slot, local, giver, turned, east, north):
    in_row = row_rank(mine)
    kept = mine & (in_row < ROW_CAP)
    rank = group_rank(kept, turned)
    kept = kept & (rank < CAP)
    place_at = turned * STRIPE + (rank >> 2) * 8 + (rank & 3)
    code = slot | (local << 3) | (giver << 8) | (place_at << 13) | (1 << 22)
    rank = row_rank(kept)
    code, east, north = pack_rows(kept, rank, [code, east, north])
    rows, positions = code.shape[0], Z * STRIPE
    place_at = jnp.where(code >= (1 << 22), (code >> 13) & 511, -1)
    lane = lax.broadcasted_iota(jnp.int32, (rows, positions), 1)
    words = jnp.zeros((rows, positions), jnp.int32)
    easts = jnp.zeros((rows, positions), jnp.float32)
    norths = jnp.zeros((rows, positions), jnp.float32)
    for j in range(ROW_CAP):
        hit = place_at[:, j : j + 1] == lane
        words = words + jnp.where(hit, code[:, j : j + 1], 0)
        easts = easts + jnp.where(hit, east[:, j : j + 1], 0.0)
        norths = norths + jnp.where(hit, north[:, j : j + 1], 0.0)
    words, easts, norths = [jnp.sum(v, axis=0, keepdims=True) for v in (words, easts, norths)]
    return words, jnp.where(words >= (1 << 22), easts, 1e5), norths, mine & ~kept


def pair_sums(gram, offsets, shifts):
    amount = len(shifts)
    squares = []
    for e, n in shifts:
        de, dn = e + offsets[0], n + offsets[1]
        squares.append(de * de + dn * dn)
    taps = gaspari_cohn(jnp.concatenate(squares)).astype(jnp.bfloat16).astype(jnp.float32)
    left, right = taps[:, :LANES], taps[:, LANES:]
    lane = lax.broadcasted_iota(jnp.int32, left.shape, 1)
    sums = [jnp.zeros(left.shape, jnp.float32) for _ in range(2)]

    def rows(k, side):
        return gram[:, k, :, LANES * side : LANES * side + LANES].reshape(left.shape)

    for k in range(8):
        low = lane < 16 * k
        a, b = turn(left, 16 * k), turn(right, 16 * k)
        middle = jnp.where(low, a, b)
        first = jnp.where(low, 0.0, a)
        last = jnp.where(low, b, 0.0)
        sums[0] = sums[0] + (middle * rows(k, 0) + first * rows(8 + k, 0))
        sums[1] = sums[1] + (last * rows(k, 1) + middle * rows(8 + k, 1))
    sums = jnp.concatenate([jnp.sum(s.reshape(amount, SIDE, LANES), axis=1) for s in sums], axis=1)
    return sums


def products(give, take):
    gram = lax.dot_general(give, take, (((0,), (0,)), ((), ())), preferred_element_type=jnp.float32)
    return gram.reshape(SIDE, SIDE, BLOCK)


def gather_kernel(
    blocks, ensemble, control, small, live, home, local, offsets, *refs,
):
    weighted, refs = refs[:Z], refs[Z:]
    taking, part_out, table, found, extra, east, north = refs[:7]
    (
        seen, counts, words, shifts, words_s, shifts_s, row_sums, gram, local_sem,
        z_send, z_recv, x_send, x_recv, core_send, core_recv, row_send, row_recv, col_send, col_recv,
    ) = refs[7:]
    col, z, x, core = place()
    member_rows, columns = ensemble.shape
    half = blocks // 2
    level = (lax.axis_index("mem") * member_rows) // MEMBERS
    scale = jnp.zeros((1, columns), jnp.float32)
    for l in range(LEVELS):
        scale = jnp.where(level == l, control[l : l + 1, :].astype(jnp.float32), scale)
    for b in range(blocks):
        own = ensemble[:, b * BLOCK : (b + 1) * BLOCK]
        taking[b] = own
        weighted[0][b] = (own.astype(jnp.float32) * scale[:, b * BLOCK : (b + 1) * BLOCK]).astype(jnp.bfloat16)
    seen[pl.ds(pl.multiple_of(col * 8, 8), 8), :] = small[...]
    counts[pl.ds(pl.multiple_of(col * 8, 8), 8), :] = live[...]

    enter([row_peer(z, x, core, s) for s in range(1, XC)] + [column_peer(col, z, s) for s in range(1, Z)])

    sent = []

    def send(source, target, send_sem, recv_sem, peer):
        copy = pltpu.make_async_remote_copy(
            src_ref=source, dst_ref=target, send_sem=send_sem, recv_sem=recv_sem,
            device_id=peer, device_id_type=MESH_ID,
        )
        copy.start()
        sent.append(copy)
        return copy

    def part(ref, slot, c):
        return ref.at[pl.ds(slot * blocks + c * half, half)]

    def send_z(way, step, c):
        sign = 1 if way == 0 else -1
        return send(
            part(weighted[(-sign * step) % Z], 0, c), part(weighted[(-sign * (step + 1)) % Z], 0, c),
            z_send.at[way, step, c], z_recv.at[way, step, c], column_peer(col, z, sign % Z),
        )

    def send_x(way, step, c):
        sign = 1 if way == 0 else -1
        return send(
            part(taking, (-sign * step) % X * 2, c), part(taking, (-sign * (step + 1)) % X * 2, c),
            x_send.at[way, step, c], x_recv.at[way, step, c], row_peer(z, x, core, sign % X * 2),
        )

    def send_core(turned, c):
        return send(
            part(taking, turned * 2, c), part(taking, turned * 2 + 1, c),
            core_send.at[turned, c], core_recv.at[turned, c], row_peer(z, x, core, 1),
        )

    row_copies = []
    for i, ref in enumerate((seen, counts)):
        rows = ref.at[pl.ds(pl.multiple_of(col * 8, 8), 8), :]
        for s in range(1, XC):
            row_copies.append(send(rows, rows, row_send.at[i, s], row_recv.at[i, s], row_peer(z, x, core, s)))
    zs, xs, cores = {}, {}, []
    for c in range(2):
        for way in range(2):
            zs[way, 0, c] = send_z(way, 0, c)
            xs[way, 0, c] = send_x(way, 0, c)
    for c in range(2):
        cores.append(send_core(0, c))
    for copy in row_copies:
        copy.wait_recv()
    col_copies = []
    for i, ref in enumerate((seen, counts)):
        rows = ref.at[pl.ds(pl.multiple_of(z * 64, 64), 64), :]
        for s in range(1, Z):
            col_copies.append(send(rows, rows, col_send.at[i, s], col_recv.at[i, s], column_peer(col, z, s)))

    def arrivals(step, c):
        for way in range(2):
            if step < 3 or c == way:
                zs[way, step, c].wait_recv()
                if step < 2 or (step == 2 and c == way):
                    zs[way, step + 1, c] = send_z(way, step + 1, c)
        for way in range(2):
            turned = (-(1 if way == 0 else -1) * (step + 1)) % X
            if step == 0 or (step == 1 and c == way):
                xs[way, step, c].wait_recv()
                if step == 0 and c == way:
                    xs[way, 1, c] = send_x(way, 1, c)
                cores.append(send_core(turned, c))

    def lists():
        for copy in col_copies:
            copy.wait_recv()
        owners = seen.shape[0] // 8
        rows = [seen[pl.ds(i, owners, stride=8), :] for i in range(4)]
        east[...] = jnp.concatenate(rows[0:2], axis=1)
        north[...] = jnp.concatenate(rows[2:4], axis=1)
        count = counts[pl.ds(0, owners, stride=8), :]
        count = jnp.concatenate([count, count], axis=1)
        mine, slot, giver, turned = own_entries(home[...], local[...], count, z, x, core)
        lane = lax.broadcasted_iota(jnp.int32, mine.shape, 1)
        word, shift_e, shift_n, left = make_lists(mine, slot, local[...], giver, turned, east[...], north[...])
        words[...] = jnp.broadcast_to(word, words.shape)
        shifts[0:1, :] = shift_e
        shifts[1:2, :] = shift_n
        receiver = slot * blocks + local[...]
        rank = row_rank(left)
        word = receiver | ((turned * blocks + giver) << 8) | (lane << 16)
        table[...] = pack_rows(left, rank, [word])[0]
        amount = jnp.max(rank, axis=1, keepdims=True) + 1
        found[...] = jnp.broadcast_to(amount, found.shape)
        extra[...] = jnp.broadcast_to(jnp.max(amount, axis=0, keepdims=True), extra.shape)
        copies = [
            pltpu.make_async_copy(words, words_s, local_sem.at[0]),
            pltpu.make_async_copy(shifts, shifts_s, local_sem.at[1]),
        ]
        for copy in copies:
            copy.start()
        for copy in copies:
            copy.wait()

    def work(turned):
        def some(n, carry):
            pairs = []
            for g in range(GROUP):
                at = turned * STRIPE + n * 8 + g
                word = words_s[0, at]
                gram[g] = products(
                    weighted[turned][(word >> 8) & 31], taking[(word & 7) * blocks + ((word >> 3) & 31)]
                )
                pairs.append((shifts_s[0, at], shifts_s[1, at]))
            sums = pair_sums(gram, offsets, pairs)
            row_sums[turned * (STRIPE // 8) + n] = jnp.concatenate([sums, jnp.zeros((8 - GROUP, BLOCK), jnp.float32)])
            return carry

        lax.fori_loop(0, STRIPE // 8, some, 0)

    arrivals(0, 0)
    arrivals(0, 1)
    lists()
    arrivals(1, 0)
    arrivals(1, 1)
    for copy in cores:
        copy.wait_recv()
    work(0)
    work(7)
    arrivals(2, 0)
    work(1)
    work(6)
    arrivals(2, 1)
    work(2)
    work(5)
    work(3)
    arrivals(3, 0)
    arrivals(3, 1)
    work(4)
    count = part_out.shape[0]
    taken = (words[0:1, :] & 7) * blocks + ((words[0:1, :] >> 3) & 31)
    hot = (lax.broadcasted_iota(jnp.int32, (count, taken.shape[1]), 0) == taken).astype(jnp.float32)
    part_out[...] = jnp.dot(
        hot, row_sums[...].reshape(taken.shape[1], BLOCK),
        preferred_element_type=jnp.float32, precision=lax.Precision.HIGHEST,
    )
    for copy in sent:
        copy.wait_send()


def extra_kernel(blocks, extra, part, table, found, east, north, offsets, *refs):
    weighted, taking, out = refs[:Z], refs[Z], refs[Z + 1]
    table_s, found_s, east_s, north_s, gram, sems = refs[Z + 2 :]
    out[...] = part[...]

    @pl.when(extra[0, 0] > 0)
    def _():
        copies = [
            pltpu.make_async_copy(a, b, sems.at[i])
            for i, (a, b) in enumerate([(table, table_s), (found, found_s), (east, east_s), (north, north_s)])
        ]
        for copy in copies:
            copy.start()
        for copy in copies:
            copy.wait()

        def row_step(row, carry):
            def entry_step(k, carry):
                word = table_s[row, k]
                receiver, giver, lane = word & 0xFF, (word >> 8) & 0xFF, word >> 16
                take = taking[receiver]
                from_slot = giver // blocks
                for t in range(Z):

                    @pl.when(from_slot == t)
                    def _():
                        gram[0] = products(weighted[t][giver - t * blocks], take)

                sums = pair_sums(gram, offsets, [(east_s[row, lane], north_s[row, lane])])
                out[pl.ds(receiver, 1), :] += sums
                return carry

            return lax.fori_loop(0, found_s[row, 0], entry_step, carry)

        lax.fori_loop(0, table.shape[0], row_step, 0)


def sum_kernel(part, out, rows_in, mine, pieces, row_send, row_recv, mem_send, mem_recv):
    _, z, x, core = place()
    mem = lax.axis_index("mem")
    mems = mine.shape[0]

    def mem_peer(step):
        return {"mem": lax.rem(mem + step, mems)}

    enter([row_peer(z, x, core, s) for s in range(1, XC)] + [mem_peer(s) for s in range(1, mems)])
    copies = []
    for s in range(1, XC):
        copy = pltpu.make_async_remote_copy(
            src_ref=part.at[s], dst_ref=rows_in.at[mirrored(s)],
            send_sem=row_send.at[s], recv_sem=row_recv.at[mirrored(s)],
            device_id=row_peer(z, x, core, s), device_id_type=MESH_ID,
        )
        copy.start()
        copies.append(copy)
    summed = part[0]
    for s in range(1, XC):
        copies[s - 1].wait()
    for s in range(1, XC):
        summed = summed + rows_in[s]
    each = summed.shape[0] // mems
    for m in range(mems):
        mine[m, :each, :] = summed[m * each : (m + 1) * each, :]
        mine[m, each:, :] = jnp.zeros((mine.shape[1] - each, BLOCK), jnp.float32)
    pieces[mem] = mine[mem]
    copies = []
    for s in range(1, mems):
        copy = pltpu.make_async_remote_copy(
            src_ref=mine.at[lax.rem(mem + s, mems)], dst_ref=pieces.at[mem],
            send_sem=mem_send.at[s], recv_sem=mem_recv.at[s],
            device_id=mem_peer(s), device_id_type=MESH_ID,
        )
        copy.start()
        copies.append(copy)
    for copy in copies:
        copy.wait()
    for l in range(LEVELS):
        first = l * (mems // LEVELS)
        both = pieces[first]
        for m in range(first + 1, first + mems // LEVELS):
            both = both + pieces[m]
        both = both / (MEMBERS - 1.0)
        for i in range(each):
            out[l : l + 1, i * BLOCK : (i + 1) * BLOCK] = both[i : i + 1, :]


def shards(ensemble, control, pair_home, pair_local, pair_count, pair_shift):
    member_rows, columns = ensemble.shape
    blocks = columns // BLOCK
    owners = lax.axis_size("col")
    mems = lax.axis_size("mem")
    entries = 2 * pair_shift.shape[1]
    sign = jnp.asarray(np.array([1.0, -1.0], np.float32))
    both = (pair_shift[:, :, None] * sign).reshape(2, entries)
    small = jnp.concatenate([both.reshape(4, LANES), jnp.zeros((4, LANES), jnp.float32)])
    live = jnp.broadcast_to(pair_count[:, None], (8, LANES))
    home = pair_home.reshape(owners, entries)
    local = pair_local.reshape(owners, entries)
    offsets = lattice_offsets()
    smem = pl.BlockSpec(memory_space=pltpu.SMEM)
    vmem = pl.BlockSpec(memory_space=pltpu.VMEM)
    dma = pltpu.SemaphoreType.DMA
    shape = jax.ShapeDtypeStruct
    positions = Z * STRIPE

    *weighted, taking, part, table, found, extra, east, north = pl.pallas_call(
        functools.partial(gather_kernel, blocks),
        out_shape=[shape((blocks, member_rows, BLOCK), jnp.bfloat16)] * Z + [
            shape((XC * blocks, member_rows, BLOCK), jnp.bfloat16),
            shape((XC * blocks, BLOCK), jnp.float32),
            shape(home.shape, jnp.int32),
            shape((owners, LANES), jnp.int32),
            shape((8, LANES), jnp.int32),
            shape(home.shape, jnp.float32),
            shape(home.shape, jnp.float32),
        ],
        in_specs=[vmem] * 7,
        out_specs=[vmem] * (Z + 7),
        scratch_shapes=[
            pltpu.VMEM((owners * 8, LANES), jnp.float32),
            pltpu.VMEM((owners * 8, LANES), jnp.int32),
            pltpu.VMEM((8, positions), jnp.int32),
            pltpu.VMEM((8, positions), jnp.float32),
            pltpu.SMEM((8, positions), jnp.int32),
            pltpu.SMEM((8, positions), jnp.float32),
            pltpu.VMEM((positions // 8, 8, BLOCK), jnp.float32),
            pltpu.VMEM((GROUP, SIDE, SIDE, BLOCK), jnp.float32),
            dma((2,)),
            dma((2, 4, 2)), dma((2, 4, 2)), dma((2, 2, 2)), dma((2, 2, 2)), dma((X, 2)), dma((X, 2)),
            dma((2, XC)), dma((2, XC)), dma((2, Z)), dma((2, Z)),
        ],
        compiler_params=pltpu.CompilerParams(
            collective_id=0, has_side_effects=True, vmem_limit_bytes=28 * 1024 * 1024
        ),
    )(ensemble, control, small, live, home, local, offsets)

    part = pl.pallas_call(
        functools.partial(extra_kernel, blocks),
        out_shape=shape(part.shape, part.dtype),
        in_specs=[smem] + [vmem] * (Z + 7),
        out_specs=vmem,
        scratch_shapes=[
            pltpu.SMEM(table.shape, jnp.int32), pltpu.SMEM(found.shape, jnp.int32),
            pltpu.SMEM(east.shape, jnp.float32), pltpu.SMEM(north.shape, jnp.float32),
            pltpu.VMEM((1, SIDE, SIDE, BLOCK), jnp.float32),
            dma((4,)),
        ],
        compiler_params=pltpu.CompilerParams(vmem_limit_bytes=24 * 1024 * 1024),
    )(extra, part, table, found, east, north, offsets, *weighted, taking)
    part = part.reshape(XC, blocks, BLOCK)

    return pl.pallas_call(
        sum_kernel,
        out_shape=jax.ShapeDtypeStruct((LEVELS, columns // mems), jnp.float32),
        in_specs=[vmem],
        out_specs=vmem,
        scratch_shapes=[
            pltpu.VMEM((XC, blocks, BLOCK), jnp.float32),
            pltpu.VMEM((mems, 8, BLOCK), jnp.float32),
            pltpu.VMEM((mems, 8, BLOCK), jnp.float32),
            dma((XC,)), dma((XC,)), dma((mems,)), dma((mems,)),
        ],
        compiler_params=pltpu.CompilerParams(
            collective_id=1, has_side_effects=True, vmem_limit_bytes=8 * 1024 * 1024
        ),
    )(part)


def solution(mesh):
    return jax.shard_map(
        shards,
        mesh=mesh,
        in_specs=(P("mem", "col"), P(None, "col"), P(), P(), P("col"), P(None, "col")),
        out_specs=P(None, ("col", "mem")),
        check_vma=False,
    )
```

time: 103 us -> 104 us (level)
    pallas_call x1, Pallas kernels: 14.2 us -> 20.8 us  [shards(): pl.pallas_call(sum_kernel, out_shape=jax.ShapeDtypeStruct((LEVELS, column...]
    pallas_call x2, Pallas kernels: 80.4 us -> 74.5 us  [the longest x1 73.8 us: shards(): pl.pallas_call(functools.partial(gather_kernel, blocks), out_shape=[shape...]
where the time goes in v3:
time: 104 us; the launch traced here: 103 us
  Pallas kernels  95.3 us (92%)
  local copies, waits for them, and re-layouts  4.72 us (5%)
  other arithmetic  2.43 us (2%)
    pallas_call x1, Pallas kernels, shards(): pl.pallas_call(functools.partial(gather_kernel, blocks), out_shape=[shape...  73.8 us
    pallas_call x1, Pallas kernels, shards(): pl.pallas_call(sum_kernel, out_shape=jax.ShapeDtypeStruct((LEVELS, column...  20.8 us
    unnamed x8, local copies, waits for them, and re-layouts  3.7 us

profile of v3, /device:TPU:1, one launch (start us, length us, event | category | flops | bytes accessed | tf_op | source)
XLA Modules:
  0.0 103.2 jit_solution(1477086925483984165)
XLA Ops:
  0.7 0.5 broadcast.9
  1.2 1.6 %reduce.3 = s32[16384]{0:T(1024)S(1)} reduce(s32[16384,1]{0,1:T(1,128)} %param.10, s32[]{:T(128)} %broadcast.9), dimensions={1}, to_apply=%param.10.reduce_sub_computation.3 | reduce | bytes 131076 | tf_op args[2]
  2.8 0.9 reshape.16.local
  3.7 0.8 broadcast_multiply_fusion
  4.5 0.1 mul.20
  4.7 0.0 copy-start
  4.7 1.0 copy-done
  5.7 0.0 copy-start.1
  5.7 0.8 copy-done.1
  6.5 0.0 copy-start.2
  6.5 0.8 copy-done.2
  7.3 73.8 %shard_map.82 = (bf16[24,40,256]{2,1,0:T(8,128)(2,1)S(1)}, bf16[24,40,256]{2,1,0:T(8,128)(2,1)S(1)}, bf16[24,40,256]{2,1,0:T(8,128)(2,1)S(1)}, bf16[24,40,256]{2...) custom-call(bf16[40,6144]{1,0:T(8,128)(2,1)S(1)} %copy-done, ...), custom_call_target="tpu_custom_call" | custom-call | tf_op jit(solution)/shard_map/pallas_call | solution.py:466
  81.1 0.7 shard_map.83
  81.8 20.8 %shard_map.84 = f32[4,768]{1,0:T(4,128)S(1)} custom-call(f32[8,24,256]{2,1,0:T(8,128)S(1)} %bitcast.4), custom_call_target="tpu_custom_call" | custom-call | tf_op jit(solution)/shard_map/pallas_call | solution.py:512
  102.6 0.6 copy.11
  (3 shorter events, 0.0 us)
Async XLA Ops:
  4.7 1.0 %copy-start = (bf16[40,6144]{1,0:T(8,128)(2,1)S(1)}, bf16[40,6144]{1,0:T(8,128)(2,1)}, u32[]{:S(2)}) copy-start(bf16[40,6144]{1,0:T(8,128)(2,1)} %ensemble.1) | copy-start | bytes 1474564
  5.7 0.8 copy-start.1
  6.5 0.8 copy-start.2

commit v4 on v3

--- a/solution.py
+++ b/solution.py
@@ -15,14 +15,18 @@
 SPACING_KM = 200.0
 HALF_WIDTH = 250.0
 XC = 8
-CAP = 32
-ROW_CAP = 16
-STRIPE = 2 * CAP
 Z = 8
 X = 4
-GROUP = 4
+LANES = 128
+BATCH = 4
+GROUP = 8
+ROW_CAP = 16
+SLOTS = ((0, 7, 1, 6, 2), (5, 3), (4,))
+CAPS = (160, 80, 48)
+STARTS = (0, 160, 240)
+POSITIONS = 384
+USED = 1 << 25
 MESH_ID = pl.DeviceIdType.MESH
-LANES = 128
 
 
 def gaspari_cohn(squared):
@@ -39,12 +43,12 @@
     return jnp.where(scaled <= 1.0, near_part, jnp.where(scaled <= 2.0, far_part, 0.0))
 
 
-def lattice_offsets():
-    giver = np.arange(SIDE)[:, None]
-    lane = np.arange(BLOCK)[None, :]
-    east = (giver - lane % SIDE) * SPACING_KM
-    north = (SIDE // 2 - lane // SIDE) * SPACING_KM + 0 * giver
-    return jnp.asarray(np.stack([east, north]).astype(np.float32))
+def tap_rows(east, north):
+    shape = (east.shape[0] if east.ndim else 1, BLOCK)
+    lane = lax.broadcasted_iota(jnp.int32, shape, 1) + SIDE // 2
+    de = east - SPACING_KM * ((lane & (SIDE - 1)) - SIDE // 2).astype(jnp.float32)
+    dn = north + SPACING_KM * (SIDE // 2 - (lane >> 4)).astype(jnp.float32)
+    return gaspari_cohn(de * de + dn * dn).astype(jnp.bfloat16).astype(jnp.float32)
 
 
 def place():
@@ -84,6 +88,13 @@
     slot = ((((home >> 1) & 3) - x) & 3) * 2 + ((home ^ core) & 1)
     turned = ((other_home >> 3) - z) & 7
     return mine, slot, other_local, turned
+
+
+def by_slot(turned, values):
+    found = jnp.zeros_like(turned)
+    for t, value in values.items():
+        found = jnp.where(turned == t, value, found)
+    return found
 
 
 def row_rank(mine):
@@ -110,13 +121,13 @@
     return arrays
 
 
-def group_rank(mine, turned):
+def group_rank(mine, group):
     rows, lanes = mine.shape
     line = lax.broadcasted_iota(jnp.int32, (rows, lanes), 0)
     lane = lax.broadcasted_iota(jnp.int32, (rows, lanes), 1)
     rank = jnp.zeros((rows, lanes), jnp.int32)
-    for t in range(0, Z, 2):
-        low, high = mine & (turned == t), mine & (turned == t + 1)
+    for t in range(0, len(CAPS), 2):
+        low, high = mine & (group == t), mine & (group == t + 1)
         upto = low.astype(jnp.int32) + (high.astype(jnp.int32) << 16)
         step = 1
         while step < lanes:
@@ -133,54 +144,58 @@
     return rank
 
 
-def make_lists(mine, slot, local, giver, turned, east, north):
+def make_lists(mine, slot, local, giver, turned, east, north, blocks):
     in_row = row_rank(mine)
     kept = mine & (in_row < ROW_CAP)
-    rank = group_rank(kept, turned)
-    kept = kept & (rank < CAP)
-    place_at = turned * STRIPE + (rank >> 2) * 8 + (rank & 3)
-    code = slot | (local << 3) | (giver << 8) | (place_at << 13) | (1 << 22)
+    group = by_slot(turned, {t: g for g, slots in enumerate(SLOTS) for t in slots})
+    rank = group_rank(kept, group)
+    kept = kept & (rank < by_slot(group, dict(enumerate(CAPS))))
+    place_at = by_slot(group, dict(enumerate(STARTS))) + rank
+    giver = giver + by_slot(turned, {t: i * blocks for slots in SLOTS for i, t in enumerate(slots)})
+    code = slot | (local << 3) | (giver << 8) | (place_at << 15) | USED
     rank = row_rank(kept)
     code, east, north = pack_rows(kept, rank, [code, east, north])
-    rows, positions = code.shape[0], Z * STRIPE
-    place_at = jnp.where(code >= (1 << 22), (code >> 13) & 511, -1)
-    lane = lax.broadcasted_iota(jnp.int32, (rows, positions), 1)
-    words = jnp.zeros((rows, positions), jnp.int32)
-    easts = jnp.zeros((rows, positions), jnp.float32)
-    norths = jnp.zeros((rows, positions), jnp.float32)
+    rows = code.shape[0]
+    place_at = jnp.where(code >= USED, (code >> 15) & 1023, -1)
+    lane = lax.broadcasted_iota(jnp.int32, (rows, POSITIONS), 1)
+    words = jnp.zeros((rows, POSITIONS), jnp.int32)
+    easts = jnp.zeros((rows, POSITIONS), jnp.float32)
+    norths = jnp.zeros((rows, POSITIONS), jnp.float32)
     for j in range(ROW_CAP):
         hit = place_at[:, j : j + 1] == lane
         words = words + jnp.where(hit, code[:, j : j + 1], 0)
         easts = easts + jnp.where(hit, east[:, j : j + 1], 0.0)
         norths = norths + jnp.where(hit, north[:, j : j + 1], 0.0)
     words, easts, norths = [jnp.sum(v, axis=0, keepdims=True) for v in (words, easts, norths)]
-    return words, jnp.where(words >= (1 << 22), easts, 1e5), norths, mine & ~kept
-
-
-def pair_sums(gram, offsets, shifts):
-    amount = len(shifts)
-    squares = []
-    for e, n in shifts:
-        de, dn = e + offsets[0], n + offsets[1]
-        squares.append(de * de + dn * dn)
-    taps = gaspari_cohn(jnp.concatenate(squares)).astype(jnp.bfloat16).astype(jnp.float32)
+    return words, jnp.where(words >= USED, easts, 1e5), norths, mine & ~kept
+
+
+def pair_sums(gram, rows):
+    amount = len(rows)
+    within = lax.broadcasted_iota(jnp.int32, (SIDE, BLOCK), 1) & (SIDE - 1)
+    within = jnp.abs(within - lax.broadcasted_iota(jnp.int32, (SIDE, BLOCK), 0)) <= SIDE // 4
+    taps = jnp.concatenate([
+        jnp.where(within, pltpu.roll(jnp.broadcast_to(r, (SIDE, BLOCK)), 0, 1, stride=1, stride_axis=0), 0.0)
+        for r in rows
+    ])
     left, right = taps[:, :LANES], taps[:, LANES:]
     lane = lax.broadcasted_iota(jnp.int32, left.shape, 1)
     sums = [jnp.zeros(left.shape, jnp.float32) for _ in range(2)]
 
-    def rows(k, side):
+    def part(k, side):
         return gram[:, k, :, LANES * side : LANES * side + LANES].reshape(left.shape)
 
     for k in range(8):
         low = lane < 16 * k
         a, b = turn(left, 16 * k), turn(right, 16 * k)
         middle = jnp.where(low, a, b)
-        first = jnp.where(low, 0.0, a)
-        last = jnp.where(low, b, 0.0)
-        sums[0] = sums[0] + (middle * rows(k, 0) + first * rows(8 + k, 0))
-        sums[1] = sums[1] + (last * rows(k, 1) + middle * rows(8 + k, 1))
-    sums = jnp.concatenate([jnp.sum(s.reshape(amount, SIDE, LANES), axis=1) for s in sums], axis=1)
-    return sums
+        sums[0] = sums[0] + middle * part(k, 0)
+        sums[1] = sums[1] + middle * part(8 + k, 1)
+        if k < 4:
+            sums[0] = sums[0] + jnp.where(low, 0.0, a) * part(8 + k, 0)
+        else:
+            sums[1] = sums[1] + jnp.where(low, b, 0.0) * part(k, 1)
+    return jnp.concatenate([jnp.sum(s.reshape(amount, SIDE, LANES), axis=1) for s in sums], axis=1)
 
 
 def products(give, take):
@@ -189,12 +204,12 @@
 
 
 def gather_kernel(
-    blocks, ensemble, control, small, live, home, local, offsets, *refs,
+    blocks, ensemble, control, small, live, home, local, *refs,
 ):
-    weighted, refs = refs[:Z], refs[Z:]
+    givers, refs = refs[:3], refs[3:]
     taking, part_out, table, found, extra, east, north = refs[:7]
     (
-        seen, counts, words, shifts, words_s, shifts_s, row_sums, gram, local_sem,
+        seen, counts, words, taps, words_s, row_sums, gram_a, gram_b, local_sem,
         z_send, z_recv, x_send, x_recv, core_send, core_recv, row_send, row_recv, col_send, col_recv,
     ) = refs[7:]
     col, z, x, core = place()
@@ -207,7 +222,7 @@
     for b in range(blocks):
         own = ensemble[:, b * BLOCK : (b + 1) * BLOCK]
         taking[b] = own
-        weighted[0][b] = (own.astype(jnp.float32) * scale[:, b * BLOCK : (b + 1) * BLOCK]).astype(jnp.bfloat16)
+        givers[0][b] = (own.astype(jnp.float32) * scale[:, b * BLOCK : (b + 1) * BLOCK]).astype(jnp.bfloat16)
     seen[pl.ds(pl.multiple_of(col * 8, 8), 8), :] = small[...]
     counts[pl.ds(pl.multiple_of(col * 8, 8), 8), :] = live[...]
 
@@ -227,10 +242,15 @@
     def part(ref, slot, c):
         return ref.at[pl.ds(slot * blocks + c * half, half)]
 
+    def giver_part(turned, c):
+        for ref, slots in zip(givers, SLOTS):
+            if turned in slots:
+                return part(ref, slots.index(turned), c)
+
     def send_z(way, step, c):
         sign = 1 if way == 0 else -1
         return send(
-            part(weighted[(-sign * step) % Z], 0, c), part(weighted[(-sign * (step + 1)) % Z], 0, c),
+            giver_part(-sign * step % Z, c), giver_part(-sign * (step + 1) % Z, c),
             z_send.at[way, step, c], z_recv.at[way, step, c], column_peer(col, z, sign % Z),
         )
 
@@ -290,44 +310,48 @@
         north[...] = jnp.concatenate(rows[2:4], axis=1)
         count = counts[pl.ds(0, owners, stride=8), :]
         count = jnp.concatenate([count, count], axis=1)
-        mine, slot, giver, turned = own_entries(home[...], local[...], count, z, x, core)
+        homes = jnp.concatenate([home[pl.ds(i, owners, stride=2), :] for i in range(2)], axis=1)
+        locals_ = jnp.concatenate([local[pl.ds(i, owners, stride=2), :] for i in range(2)], axis=1)
+        mine, slot, giver, turned = own_entries(homes, locals_, count, z, x, core)
         lane = lax.broadcasted_iota(jnp.int32, mine.shape, 1)
-        word, shift_e, shift_n, left = make_lists(mine, slot, local[...], giver, turned, east[...], north[...])
+        word, shift_e, shift_n, left = make_lists(
+            mine, slot, locals_, giver, turned, east[...], north[...], blocks
+        )
         words[...] = jnp.broadcast_to(word, words.shape)
-        shifts[0:1, :] = shift_e
-        shifts[1:2, :] = shift_n
-        receiver = slot * blocks + local[...]
+        copy = pltpu.make_async_copy(words, words_s, local_sem.at[0])
+        copy.start()
+        shift = jnp.concatenate([shift_e, shift_n, jnp.zeros((6, POSITIONS), jnp.float32)]).T
+        for at in range(0, POSITIONS, LANES):
+            taps[at : at + LANES, :] = tap_rows(shift[at : at + LANES, 0:1], shift[at : at + LANES, 1:2])
+        receiver = slot * blocks + locals_
         rank = row_rank(left)
-        word = receiver | ((turned * blocks + giver) << 8) | (lane << 16)
-        table[...] = pack_rows(left, rank, [word])[0]
+        table[...] = pack_rows(left, rank, [receiver | (turned << 8) | (giver << 11) | (lane << 16)])[0]
         amount = jnp.max(rank, axis=1, keepdims=True) + 1
         found[...] = jnp.broadcast_to(amount, found.shape)
         extra[...] = jnp.broadcast_to(jnp.max(amount, axis=0, keepdims=True), extra.shape)
-        copies = [
-            pltpu.make_async_copy(words, words_s, local_sem.at[0]),
-            pltpu.make_async_copy(shifts, shifts_s, local_sem.at[1]),
-        ]
-        for copy in copies:
-            copy.start()
-        for copy in copies:
-            copy.wait()
-
-    def work(turned):
+        copy.wait()
+
+    def work(group):
+        first = STARTS[group] // GROUP
+
         def some(n, carry):
-            pairs = []
-            for g in range(GROUP):
-                at = turned * STRIPE + n * 8 + g
-                word = words_s[0, at]
-                gram[g] = products(
-                    weighted[turned][(word >> 8) & 31], taking[(word & 7) * blocks + ((word >> 3) & 31)]
-                )
-                pairs.append((shifts_s[0, at], shifts_s[1, at]))
-            sums = pair_sums(gram, offsets, pairs)
-            row_sums[turned * (STRIPE // 8) + n] = jnp.concatenate([sums, jnp.zeros((8 - GROUP, BLOCK), jnp.float32)])
+            sums = []
+            for batch, gram in enumerate((gram_a, gram_b)):
+                for g in range(BATCH):
+                    word = words_s[0, n * GROUP + batch * BATCH + g]
+                    gram[g] = products(
+                        givers[group][(word >> 8) & 127], taking[(word & 7) * blocks + ((word >> 3) & 31)]
+                    )
+            rows = taps[pl.ds(pl.multiple_of(n * GROUP, GROUP), GROUP), :]
+            for batch, gram in enumerate((gram_a, gram_b)):
+                at = batch * BATCH
+                sums.append(pair_sums(gram, [rows[at + g : at + g + 1, :] for g in range(BATCH)]))
+            row_sums[n] = jnp.concatenate(sums)
             return carry
 
-        lax.fori_loop(0, STRIPE // 8, some, 0)
-
+        lax.fori_loop(first, first + CAPS[group] // GROUP, some, 0)
+
+    row_sums[...] = jnp.zeros_like(row_sums)
     arrivals(0, 0)
     arrivals(0, 1)
     lists()
@@ -336,17 +360,12 @@
     for copy in cores:
         copy.wait_recv()
     work(0)
-    work(7)
     arrivals(2, 0)
+    arrivals(2, 1)
     work(1)
-    work(6)
-    arrivals(2, 1)
-    work(2)
-    work(5)
-    work(3)
     arrivals(3, 0)
     arrivals(3, 1)
-    work(4)
+    work(2)
     count = part_out.shape[0]
     taken = (words[0:1, :] & 7) * blocks + ((words[0:1, :] >> 3) & 31)
     hot = (lax.broadcasted_iota(jnp.int32, (count, taken.shape[1]), 0) == taken).astype(jnp.float32)
@@ -358,9 +377,8 @@
         copy.wait_send()
 
 
-def extra_kernel(blocks, extra, part, table, found, east, north, offsets, *refs):
-    weighted, taking, out = refs[:Z], refs[Z], refs[Z + 1]
-    table_s, found_s, east_s, north_s, gram, sems = refs[Z + 2 :]
+def extra_kernel(blocks, extra, part, table, found, east, north, near, middle, far, taking, *refs):
+    out, table_s, found_s, east_s, north_s, gram, sems = refs
     out[...] = part[...]
 
     @pl.when(extra[0, 0] > 0)
@@ -377,17 +395,16 @@
         def row_step(row, carry):
             def entry_step(k, carry):
                 word = table_s[row, k]
-                receiver, giver, lane = word & 0xFF, (word >> 8) & 0xFF, word >> 16
+                receiver, turned, giver, lane = word & 255, (word >> 8) & 7, (word >> 11) & 31, word >> 16
                 take = taking[receiver]
-                from_slot = giver // blocks
-                for t in range(Z):
-
-                    @pl.when(from_slot == t)
-                    def _():
-                        gram[0] = products(weighted[t][giver - t * blocks], take)
-
-                sums = pair_sums(gram, offsets, [(east_s[row, lane], north_s[row, lane])])
-                out[pl.ds(receiver, 1), :] += sums
+                for ref, slots in zip((near, middle, far), SLOTS):
+                    for i, t in enumerate(slots):
+
+                        @pl.when(turned == t)
+                        def _():
+                            gram[0] = products(ref[i * blocks + giver], take)
+
+                out[pl.ds(receiver, 1), :] += pair_sums(gram, [tap_rows(east_s[row, lane], north_s[row, lane])])
                 return carry
 
             return lax.fori_loop(0, found_s[row, 0], entry_step, carry)
@@ -454,50 +471,48 @@
     both = (pair_shift[:, :, None] * sign).reshape(2, entries)
     small = jnp.concatenate([both.reshape(4, LANES), jnp.zeros((4, LANES), jnp.float32)])
     live = jnp.broadcast_to(pair_count[:, None], (8, LANES))
-    home = pair_home.reshape(owners, entries)
-    local = pair_local.reshape(owners, entries)
-    offsets = lattice_offsets()
+    home = pair_home.reshape(-1, LANES)
+    local = pair_local.reshape(-1, LANES)
     smem = pl.BlockSpec(memory_space=pltpu.SMEM)
     vmem = pl.BlockSpec(memory_space=pltpu.VMEM)
     dma = pltpu.SemaphoreType.DMA
     shape = jax.ShapeDtypeStruct
-    positions = Z * STRIPE
-
-    *weighted, taking, part, table, found, extra, east, north = pl.pallas_call(
+
+    *givers, taking, part, table, found, extra, east, north = pl.pallas_call(
         functools.partial(gather_kernel, blocks),
-        out_shape=[shape((blocks, member_rows, BLOCK), jnp.bfloat16)] * Z + [
+        out_shape=[shape((len(slots) * blocks, member_rows, BLOCK), jnp.bfloat16) for slots in SLOTS] + [
             shape((XC * blocks, member_rows, BLOCK), jnp.bfloat16),
             shape((XC * blocks, BLOCK), jnp.float32),
-            shape(home.shape, jnp.int32),
+            shape((owners, entries), jnp.int32),
             shape((owners, LANES), jnp.int32),
             shape((8, LANES), jnp.int32),
-            shape(home.shape, jnp.float32),
-            shape(home.shape, jnp.float32),
+            shape((owners, entries), jnp.float32),
+            shape((owners, entries), jnp.float32),
         ],
-        in_specs=[vmem] * 7,
-        out_specs=[vmem] * (Z + 7),
+        in_specs=[vmem] * 6,
+        out_specs=[vmem] * 10,
         scratch_shapes=[
             pltpu.VMEM((owners * 8, LANES), jnp.float32),
             pltpu.VMEM((owners * 8, LANES), jnp.int32),
-            pltpu.VMEM((8, positions), jnp.int32),
-            pltpu.VMEM((8, positions), jnp.float32),
-            pltpu.SMEM((8, positions), jnp.int32),
-            pltpu.SMEM((8, positions), jnp.float32),
-            pltpu.VMEM((positions // 8, 8, BLOCK), jnp.float32),
-            pltpu.VMEM((GROUP, SIDE, SIDE, BLOCK), jnp.float32),
-            dma((2,)),
+            pltpu.VMEM((8, POSITIONS), jnp.int32),
+            pltpu.VMEM((POSITIONS, BLOCK), jnp.float32),
+            pltpu.SMEM((8, POSITIONS), jnp.int32),
+            pltpu.VMEM((POSITIONS // GROUP, GROUP, BLOCK), jnp.float32),
+            pltpu.VMEM((BATCH, SIDE, SIDE, BLOCK), jnp.float32),
+            pltpu.VMEM((BATCH, SIDE, SIDE, BLOCK), jnp.float32),
+            dma((1,)),
             dma((2, 4, 2)), dma((2, 4, 2)), dma((2, 2, 2)), dma((2, 2, 2)), dma((X, 2)), dma((X, 2)),
             dma((2, XC)), dma((2, XC)), dma((2, Z)), dma((2, Z)),
         ],
         compiler_params=pltpu.CompilerParams(
             collective_id=0, has_side_effects=True, vmem_limit_bytes=28 * 1024 * 1024
         ),
-    )(ensemble, control, small, live, home, local, offsets)
+    )(ensemble, control, small, live, home, local)
 
     part = pl.pallas_call(
         functools.partial(extra_kernel, blocks),
         out_shape=shape(part.shape, part.dtype),
-        in_specs=[smem] + [vmem] * (Z + 7),
+        in_specs=[smem] + [vmem] * 9,
         out_specs=vmem,
         scratch_shapes=[
             pltpu.SMEM(table.shape, jnp.int32), pltpu.SMEM(found.shape, jnp.int32),
@@ -506,7 +521,7 @@
             dma((4,)),
         ],
         compiler_params=pltpu.CompilerParams(vmem_limit_bytes=24 * 1024 * 1024),
-    )(extra, part, table, found, east, north, offsets, *weighted, taking)
+    )(extra, part, table, found, east, north, *givers, taking)
     part = part.reshape(XC, blocks, BLOCK)
 
     return pl.pallas_call(

time: 104 us -> 94.9 us (0.913)
  Pallas kernels: 95.3 us -> 88.8 us
  other arithmetic: 2.43 us -> 0.79 us
    pallas_call x1, Pallas kernels: 20.8 us -> 14.2 us  [shards(): pl.pallas_call(sum_kernel, out_shape=jax.ShapeDtypeStruct((LEVELS, column...]
    unnamed x1 -> x0, other arithmetic: 1.64 us -> none
    unnamed x8 -> x9, local copies, waits for them, and re-layouts: 3.7 us -> 4.1 us
where the time goes in v4:
time: 94.9 us; the launch traced here: 94.6 us
  Pallas kernels  88.8 us (94%)
  local copies, waits for them, and re-layouts  4.25 us (4%)
    pallas_call x1, Pallas kernels, shards(): pl.pallas_call(functools.partial(gather_kernel, blocks), out_shape=[shape...  73.9 us
    pallas_call x1, Pallas kernels, shards(): pl.pallas_call(sum_kernel, out_shape=jax.ShapeDtypeStruct((LEVELS, column...  14.2 us
    unnamed x9, local copies, waits for them, and re-layouts  4.1 us

profile of v4, /device:TPU:1, one launch (start us, length us, event | category | flops | bytes accessed | tf_op | source)
XLA Modules:
  0.0 94.6 jit_solution(8934774352713037112)
XLA Ops:
  0.7 0.8 broadcast_multiply_fusion
  1.5 0.1 mul.20
  1.6 0.0 copy-start
  1.6 1.0 %copy-done = bf16[40,6144]{1,0:T(8,128)(2,1)S(1)} copy-done((bf16[40,6144]{1,0:T(8,128)(2,1)S(1)}, bf16[40,6144]{1,0:T(8,128)(2,1)}, u32[]{:S(2)}) %copy-start) | copy-done | bytes 491544
  2.7 0.0 copy-start.1
  2.7 0.8 copy-done.1
  3.5 0.0 copy-start.2
  3.5 0.8 copy-done.2
  4.3 0.0 copy-start.3
  4.3 0.8 copy-done.3
  5.1 73.9 %shard_map.73 = (bf16[120,40,256]{2,1,0:T(8,128)(2,1)S(1)}, bf16[48,40,256]{2,1,0:T(8,128)(2,1)S(1)}, bf16[24,40,256]{2,1,0:T(8,128)(2,1)S(1)}, bf16[192,40,256]...) custom-call(bf16[40,6144]{1,0:T(8,128)(2,1)S(1)} %copy-done, ...), custom_call_target="tpu_custom_call" | custom-call | tf_op jit(solution)/shard_map/pallas_call | solution.py:481
  79.1 0.7 shard_map.74
  79.7 14.2 %shard_map.75 = f32[4,768]{1,0:T(4,128)S(1)} custom-call(f32[8,24,256]{2,1,0:T(8,128)S(1)} %bitcast.5), custom_call_target="tpu_custom_call" | custom-call | tf_op jit(solution)/shard_map/pallas_call | solution.py:527
  94.0 0.6 copy.10
  (2 shorter events, 0.0 us)
Async XLA Ops:
  1.6 1.0 %copy-start = (bf16[40,6144]{1,0:T(8,128)(2,1)S(1)}, bf16[40,6144]{1,0:T(8,128)(2,1)}, u32[]{:S(2)}) copy-start(bf16[40,6144]{1,0:T(8,128)(2,1)} %ensemble.1) | copy-start | bytes 1474564
  2.7 0.8 copy-start.1
  3.5 0.8 copy-start.2
  4.3 0.8 copy-start.3

commit v5 on v4

--- a/solution.py
+++ b/solution.py
@@ -18,7 +18,6 @@
 Z = 8
 X = 4
 LANES = 128
-BATCH = 4
 GROUP = 8
 ROW_CAP = 16
 SLOTS = ((0, 7, 1, 6, 2), (5, 3), (4,))
@@ -68,11 +67,11 @@
     return (X - slot // 2) % X * 2 + slot % 2
 
 
-def enter(peers):
+def greet(peers):
     barrier = pltpu.get_barrier_semaphore()
     for peer in peers:
         pl.semaphore_signal(barrier, inc=1, device_id=peer, device_id_type=MESH_ID)
-    pl.semaphore_wait(barrier, len(peers))
+    return lambda: pl.semaphore_wait(barrier, len(peers))
 
 
 def turn(a, shift):
@@ -170,37 +169,31 @@
     return words, jnp.where(words >= USED, easts, 1e5), norths, mine & ~kept
 
 
-def pair_sums(gram, rows):
-    amount = len(rows)
+def taper_tile(row):
     within = lax.broadcasted_iota(jnp.int32, (SIDE, BLOCK), 1) & (SIDE - 1)
     within = jnp.abs(within - lax.broadcasted_iota(jnp.int32, (SIDE, BLOCK), 0)) <= SIDE // 4
-    taps = jnp.concatenate([
-        jnp.where(within, pltpu.roll(jnp.broadcast_to(r, (SIDE, BLOCK)), 0, 1, stride=1, stride_axis=0), 0.0)
-        for r in rows
-    ])
+    taps = pltpu.roll(jnp.broadcast_to(row, (SIDE, BLOCK)), 0, 1, stride=1, stride_axis=0)
+    taps = jnp.where(within, taps, 0.0)
     left, right = taps[:, :LANES], taps[:, LANES:]
     lane = lax.broadcasted_iota(jnp.int32, left.shape, 1)
-    sums = [jnp.zeros(left.shape, jnp.float32) for _ in range(2)]
-
-    def part(k, side):
-        return gram[:, k, :, LANES * side : LANES * side + LANES].reshape(left.shape)
-
+    none = jnp.zeros(left.shape, jnp.bfloat16)
+    upper, lower = [], []
     for k in range(8):
         low = lane < 16 * k
         a, b = turn(left, 16 * k), turn(right, 16 * k)
-        middle = jnp.where(low, a, b)
-        sums[0] = sums[0] + middle * part(k, 0)
-        sums[1] = sums[1] + middle * part(8 + k, 1)
+        middle = jnp.where(low, a, b).astype(jnp.bfloat16)
         if k < 4:
-            sums[0] = sums[0] + jnp.where(low, 0.0, a) * part(8 + k, 0)
+            upper.append(jnp.concatenate([middle, none], axis=1))
+            lower.append(jnp.concatenate([jnp.where(low, 0.0, a).astype(jnp.bfloat16), middle], axis=1))
         else:
-            sums[1] = sums[1] + jnp.where(low, b, 0.0) * part(k, 1)
-    return jnp.concatenate([jnp.sum(s.reshape(amount, SIDE, LANES), axis=1) for s in sums], axis=1)
-
-
-def products(give, take):
-    gram = lax.dot_general(give, take, (((0,), (0,)), ((), ())), preferred_element_type=jnp.float32)
-    return gram.reshape(SIDE, SIDE, BLOCK)
+            upper.append(jnp.concatenate([middle, jnp.where(low, b, 0.0).astype(jnp.bfloat16)], axis=1))
+            lower.append(jnp.concatenate([none, middle], axis=1))
+    return jnp.concatenate(upper + lower)
+
+
+def pair_sum(row, give, take):
+    reached = jnp.dot(give, taper_tile(row), preferred_element_type=jnp.float32)
+    return jnp.sum(reached * take.astype(jnp.float32), axis=0, keepdims=True)
 
 
 def gather_kernel(
@@ -209,10 +202,11 @@
     givers, refs = refs[:3], refs[3:]
     taking, part_out, table, found, extra, east, north = refs[:7]
     (
-        seen, counts, words, taps, words_s, row_sums, gram_a, gram_b, local_sem,
+        seen, counts, words, taps, words_s, row_sums, local_sem,
         z_send, z_recv, x_send, x_recv, core_send, core_recv, row_send, row_recv, col_send, col_recv,
     ) = refs[7:]
     col, z, x, core = place()
+    entered = greet([row_peer(z, x, core, s) for s in range(1, XC)] + [column_peer(col, z, s) for s in range(1, Z)])
     member_rows, columns = ensemble.shape
     half = blocks // 2
     level = (lax.axis_index("mem") * member_rows) // MEMBERS
@@ -226,7 +220,7 @@
     seen[pl.ds(pl.multiple_of(col * 8, 8), 8), :] = small[...]
     counts[pl.ds(pl.multiple_of(col * 8, 8), 8), :] = live[...]
 
-    enter([row_peer(z, x, core, s) for s in range(1, XC)] + [column_peer(col, z, s) for s in range(1, Z)])
+    entered()
 
     sent = []
 
@@ -331,37 +325,37 @@
         extra[...] = jnp.broadcast_to(jnp.max(amount, axis=0, keepdims=True), extra.shape)
         copy.wait()
 
-    def work(group):
+    def work(group, begin=0, end=None):
         first = STARTS[group] // GROUP
 
         def some(n, carry):
+            rows = taps[pl.ds(pl.multiple_of(n * GROUP, GROUP), GROUP), :]
             sums = []
-            for batch, gram in enumerate((gram_a, gram_b)):
-                for g in range(BATCH):
-                    word = words_s[0, n * GROUP + batch * BATCH + g]
-                    gram[g] = products(
-                        givers[group][(word >> 8) & 127], taking[(word & 7) * blocks + ((word >> 3) & 31)]
-                    )
-            rows = taps[pl.ds(pl.multiple_of(n * GROUP, GROUP), GROUP), :]
-            for batch, gram in enumerate((gram_a, gram_b)):
-                at = batch * BATCH
-                sums.append(pair_sums(gram, [rows[at + g : at + g + 1, :] for g in range(BATCH)]))
+            for g in range(GROUP):
+                word = words_s[0, n * GROUP + g]
+                sums.append(pair_sum(
+                    rows[g : g + 1, :],
+                    givers[group][(word >> 8) & 127], taking[(word & 7) * blocks + ((word >> 3) & 31)],
+                ))
             row_sums[n] = jnp.concatenate(sums)
             return carry
 
-        lax.fori_loop(first, first + CAPS[group] // GROUP, some, 0)
+        end = CAPS[group] if end is None else end
+        lax.fori_loop(first + begin // GROUP, first + end // GROUP, some, 0)
 
     row_sums[...] = jnp.zeros_like(row_sums)
+    lists()
     arrivals(0, 0)
     arrivals(0, 1)
-    lists()
     arrivals(1, 0)
     arrivals(1, 1)
     for copy in cores:
         copy.wait_recv()
-    work(0)
+    work(0, 0, 56)
     arrivals(2, 0)
+    work(0, 56, 112)
     arrivals(2, 1)
+    work(0, 112)
     work(1)
     arrivals(3, 0)
     arrivals(3, 1)
@@ -378,7 +372,7 @@
 
 
 def extra_kernel(blocks, extra, part, table, found, east, north, near, middle, far, taking, *refs):
-    out, table_s, found_s, east_s, north_s, gram, sems = refs
+    out, table_s, found_s, east_s, north_s, sems = refs
     out[...] = part[...]
 
     @pl.when(extra[0, 0] > 0)
@@ -396,15 +390,14 @@
             def entry_step(k, carry):
                 word = table_s[row, k]
                 receiver, turned, giver, lane = word & 255, (word >> 8) & 7, (word >> 11) & 31, word >> 16
-                take = taking[receiver]
+                line = tap_rows(east_s[row, lane], north_s[row, lane])
                 for ref, slots in zip((near, middle, far), SLOTS):
                     for i, t in enumerate(slots):
 
                         @pl.when(turned == t)
                         def _():
-                            gram[0] = products(ref[i * blocks + giver], take)
-
-                out[pl.ds(receiver, 1), :] += pair_sums(gram, [tap_rows(east_s[row, lane], north_s[row, lane])])
+                            out[pl.ds(receiver, 1), :] += pair_sum(line, ref[i * blocks + giver], taking[receiver])
+
                 return carry
 
             return lax.fori_loop(0, found_s[row, 0], entry_step, carry)
@@ -420,7 +413,7 @@
     def mem_peer(step):
         return {"mem": lax.rem(mem + step, mems)}
 
-    enter([row_peer(z, x, core, s) for s in range(1, XC)] + [mem_peer(s) for s in range(1, mems)])
+    greet([row_peer(z, x, core, s) for s in range(1, XC)] + [mem_peer(s) for s in range(1, mems)])()
     copies = []
     for s in range(1, XC):
         copy = pltpu.make_async_remote_copy(
@@ -498,8 +491,6 @@
             pltpu.VMEM((POSITIONS, BLOCK), jnp.float32),
             pltpu.SMEM((8, POSITIONS), jnp.int32),
             pltpu.VMEM((POSITIONS // GROUP, GROUP, BLOCK), jnp.float32),
-            pltpu.VMEM((BATCH, SIDE, SIDE, BLOCK), jnp.float32),
-            pltpu.VMEM((BATCH, SIDE, SIDE, BLOCK), jnp.float32),
             dma((1,)),
             dma((2, 4, 2)), dma((2, 4, 2)), dma((2, 2, 2)), dma((2, 2, 2)), dma((X, 2)), dma((X, 2)),
             dma((2, XC)), dma((2, XC)), dma((2, Z)), dma((2, Z)),
@@ -517,7 +508,6 @@
         scratch_shapes=[
             pltpu.SMEM(table.shape, jnp.int32), pltpu.SMEM(found.shape, jnp.int32),
             pltpu.SMEM(east.shape, jnp.float32), pltpu.SMEM(north.shape, jnp.float32),
-            pltpu.VMEM((1, SIDE, SIDE, BLOCK), jnp.float32),
             dma((4,)),
         ],
         compiler_params=pltpu.CompilerParams(vmem_limit_bytes=24 * 1024 * 1024),

time: 94.9 us -> 96.8 us (1.020)
  Pallas kernels: 88.8 us -> 90.7 us
    pallas_call x1, Pallas kernels: 73.9 us -> 75.3 us  [shards(): pl.pallas_call(functools.partial(gather_kernel, blocks), out_shape=[shape...]
where the time goes in v5:
time: 96.8 us; the launch traced here: 96.5 us
  Pallas kernels  90.7 us (94%)
  local copies, waits for them, and re-layouts  4.25 us (4%)
    pallas_call x1, Pallas kernels, shards(): pl.pallas_call(functools.partial(gather_kernel, blocks), out_shape=[shape...  75.3 us
    pallas_call x1, Pallas kernels, shards(): pl.pallas_call(sum_kernel, out_shape=jax.ShapeDtypeStruct((LEVELS, column...  14.8 us
    unnamed x9, local copies, waits for them, and re-layouts  4.1 us

profile of v5, /device:TPU:1, one launch (start us, length us, event | category | flops | bytes accessed | tf_op | source)
XLA Modules:
  0.0 96.5 jit_solution(10789143552995496845)
XLA Ops:
  0.7 0.8 broadcast_multiply_fusion
  1.5 0.1 mul.20
  1.6 0.0 copy-start
  1.6 1.0 %copy-done = bf16[40,6144]{1,0:T(8,128)(2,1)S(1)} copy-done((bf16[40,6144]{1,0:T(8,128)(2,1)S(1)}, bf16[40,6144]{1,0:T(8,128)(2,1)}, u32[]{:S(2)}) %copy-start) | copy-done | bytes 491544
  2.7 0.0 copy-start.1
  2.7 0.8 copy-done.1
  3.5 0.0 copy-start.2
  3.5 0.8 copy-done.2
  4.3 0.0 copy-start.3
  4.3 0.8 copy-done.3
  5.1 75.3 %shard_map.73 = (bf16[120,40,256]{2,1,0:T(8,128)(2,1)S(1)}, bf16[48,40,256]{2,1,0:T(8,128)(2,1)S(1)}, bf16[24,40,256]{2,1,0:T(8,128)(2,1)S(1)}, bf16[192,40,256]...) custom-call(bf16[40,6144]{1,0:T(8,128)(2,1)S(1)} %copy-done, ...), custom_call_target="tpu_custom_call" | custom-call | tf_op jit(solution)/shard_map/pallas_call | solution.py:474
  80.4 0.7 shard_map.74
  81.1 14.8 %shard_map.75 = f32[4,768]{1,0:T(4,128)S(1)} custom-call(f32[8,24,256]{2,1,0:T(8,128)S(1)} %bitcast.5), custom_call_target="tpu_custom_call" | custom-call | tf_op jit(solution)/shard_map/pallas_call | solution.py:517
  95.9 0.6 copy.10
  (2 shorter events, 0.0 us)
Async XLA Ops:
  1.6 1.0 %copy-start = (bf16[40,6144]{1,0:T(8,128)(2,1)S(1)}, bf16[40,6144]{1,0:T(8,128)(2,1)}, u32[]{:S(2)}) copy-start(bf16[40,6144]{1,0:T(8,128)(2,1)} %ensemble.1) | copy-start | bytes 1474564
  2.7 0.8 copy-start.1
  3.5 0.8 copy-start.2
  4.3 0.8 copy-start.3

commit v6 on v5

--- a/solution.py
+++ b/solution.py
@@ -18,11 +18,12 @@
 Z = 8
 X = 4
 LANES = 128
-GROUP = 8
+GROUP = 16
 ROW_CAP = 16
-SLOTS = ((0, 7, 1, 6, 2), (5, 3), (4,))
-CAPS = (160, 80, 48)
-STARTS = (0, 160, 240)
+SLOTS = ((0, 7, 1), (6, 2), (5, 3), (4,))
+CAPS = (112, 80, 80, 48)
+STARTS = (0, 112, 192, 272)
+EARLY = 256
 POSITIONS = 384
 USED = 1 << 25
 MESH_ID = pl.DeviceIdType.MESH
@@ -199,7 +200,7 @@
 def gather_kernel(
     blocks, ensemble, control, small, live, home, local, *refs,
 ):
-    givers, refs = refs[:3], refs[3:]
+    givers, refs = refs[: len(SLOTS)], refs[len(SLOTS) :]
     taking, part_out, table, found, extra, east, north = refs[:7]
     (
         seen, counts, words, taps, words_s, row_sums, local_sem,
@@ -281,12 +282,7 @@
         for s in range(1, Z):
             col_copies.append(send(rows, rows, col_send.at[i, s], col_recv.at[i, s], column_peer(col, z, s)))
 
-    def arrivals(step, c):
-        for way in range(2):
-            if step < 3 or c == way:
-                zs[way, step, c].wait_recv()
-                if step < 2 or (step == 2 and c == way):
-                    zs[way, step + 1, c] = send_z(way, step + 1, c)
+    def row_arrivals(step, c):
         for way in range(2):
             turned = (-(1 if way == 0 else -1) * (step + 1)) % X
             if step == 0 or (step == 1 and c == way):
@@ -295,6 +291,14 @@
                     xs[way, 1, c] = send_x(way, 1, c)
                 cores.append(send_core(turned, c))
 
+    def arrivals(step, c, rows=True):
+        if rows:
+            row_arrivals(step, c)
+        for way in range(2):
+            if step < 3 or c == way:
+                zs[way, step, c].wait_recv()
+                if step < 2 or (step == 2 and c == way):
+                    zs[way, step + 1, c] = send_z(way, step + 1, c)
     def lists():
         for copy in col_copies:
             copy.wait_recv()
@@ -348,30 +352,38 @@
     arrivals(0, 0)
     arrivals(0, 1)
     arrivals(1, 0)
-    arrivals(1, 1)
+    row_arrivals(1, 1)
     for copy in cores:
         copy.wait_recv()
-    work(0, 0, 56)
+    work(0, 0, 48)
+    arrivals(1, 1, False)
+    work(0, 48)
     arrivals(2, 0)
-    work(0, 56, 112)
+    work(1)
     arrivals(2, 1)
-    work(0, 112)
-    work(1)
+    work(2)
+
+    taken = (words[0:1, :] & 7) * blocks + ((words[0:1, :] >> 3) & 31)
+    count = part_out.shape[0]
+
+    def spread(begin, end):
+        hot = lax.broadcasted_iota(jnp.int32, (count, end - begin), 0) == taken[:, begin:end]
+        sums = row_sums[begin // GROUP : end // GROUP].reshape(end - begin, BLOCK)
+        return jnp.dot(
+            hot.astype(jnp.float32), sums, preferred_element_type=jnp.float32, precision=lax.Precision.HIGHEST
+        )
+
+    part_out[...] = spread(0, EARLY)
     arrivals(3, 0)
     arrivals(3, 1)
-    work(2)
-    count = part_out.shape[0]
-    taken = (words[0:1, :] & 7) * blocks + ((words[0:1, :] >> 3) & 31)
-    hot = (lax.broadcasted_iota(jnp.int32, (count, taken.shape[1]), 0) == taken).astype(jnp.float32)
-    part_out[...] = jnp.dot(
-        hot, row_sums[...].reshape(taken.shape[1], BLOCK),
-        preferred_element_type=jnp.float32, precision=lax.Precision.HIGHEST,
-    )
+    work(3)
+    part_out[...] += spread(EARLY, POSITIONS)
     for copy in sent:
         copy.wait_send()
 
 
-def extra_kernel(blocks, extra, part, table, found, east, north, near, middle, far, taking, *refs):
+def extra_kernel(blocks, extra, part, table, found, east, north, *refs):
+    givers, taking, refs = refs[: len(SLOTS)], refs[len(SLOTS)], refs[len(SLOTS) + 1 :]
     out, table_s, found_s, east_s, north_s, sems = refs
     out[...] = part[...]
 
@@ -391,7 +403,7 @@
                 word = table_s[row, k]
                 receiver, turned, giver, lane = word & 255, (word >> 8) & 7, (word >> 11) & 31, word >> 16
                 line = tap_rows(east_s[row, lane], north_s[row, lane])
-                for ref, slots in zip((near, middle, far), SLOTS):
+                for ref, slots in zip(givers, SLOTS):
                     for i, t in enumerate(slots):
 
                         @pl.when(turned == t)
@@ -483,7 +495,7 @@
             shape((owners, entries), jnp.float32),
         ],
         in_specs=[vmem] * 6,
-        out_specs=[vmem] * 10,
+        out_specs=[vmem] * (len(SLOTS) + 7),
         scratch_shapes=[
             pltpu.VMEM((owners * 8, LANES), jnp.float32),
             pltpu.VMEM((owners * 8, LANES), jnp.int32),
@@ -503,7 +515,7 @@
     part = pl.pallas_call(
         functools.partial(extra_kernel, blocks),
         out_shape=shape(part.shape, part.dtype),
-        in_specs=[smem] + [vmem] * 9,
+        in_specs=[smem] + [vmem] * (len(SLOTS) + 6),
         out_specs=vmem,
         scratch_shapes=[
             pltpu.SMEM(table.shape, jnp.int32), pltpu.SMEM(found.shape, jnp.int32),

time: 96.8 us -> 95.3 us (0.985)
  Pallas kernels: 90.7 us -> 89.2 us
    pallas_call x1, Pallas kernels: 75.3 us -> 71.1 us  [shards(): pl.pallas_call(functools.partial(gather_kernel, blocks), out_shape=[shape...]
    pallas_call x1, Pallas kernels: 14.8 us -> 17.5 us  [shards(): pl.pallas_call(sum_kernel, out_shape=jax.ShapeDtypeStruct((LEVELS, column...]
where the time goes in v6:
time: 95.3 us; the launch traced here: 95 us
  Pallas kernels  89.2 us (94%)
  local copies, waits for them, and re-layouts  4.25 us (4%)
    pallas_call x1, Pallas kernels, shards(): pl.pallas_call(functools.partial(gather_kernel, blocks), out_shape=[shape...  71.1 us
    pallas_call x1, Pallas kernels, shards(): pl.pallas_call(sum_kernel, out_shape=jax.ShapeDtypeStruct((LEVELS, column...  17.5 us
    unnamed x9, local copies, waits for them, and re-layouts  4.1 us

profile of v6, /device:TPU:1, one launch (start us, length us, event | category | flops | bytes accessed | tf_op | source)
XLA Modules:
  0.0 95.0 jit_solution(5950386174725268776)
XLA Ops:
  0.7 0.8 broadcast_multiply_fusion
  1.5 0.1 mul.20
  1.6 0.0 copy-start
  1.6 1.0 %copy-done = bf16[40,6144]{1,0:T(8,128)(2,1)S(1)} copy-done((bf16[40,6144]{1,0:T(8,128)(2,1)S(1)}, bf16[40,6144]{1,0:T(8,128)(2,1)}, u32[]{:S(2)}) %copy-start) | copy-done | bytes 491544
  2.7 0.0 copy-start.1
  2.7 0.8 copy-done.1
  3.5 0.0 copy-start.2
  3.5 0.8 copy-done.2
  4.3 0.0 copy-start.3
  4.3 0.8 copy-done.3
  5.1 71.1 %shard_map.73 = (bf16[72,40,256]{2,1,0:T(8,128)(2,1)S(1)}, bf16[48,40,256]{2,1,0:T(8,128)(2,1)S(1)}, bf16[48,40,256]{2,1,0:T(8,128)(2,1)S(1)}, bf16[24,40,256]{2...) custom-call(bf16[40,6144]{1,0:T(8,128)(2,1)S(1)} %copy-done, ...), custom_call_target="tpu_custom_call" | custom-call | tf_op jit(solution)/shard_map/pallas_call | solution.py:486
  76.2 0.7 shard_map.74
  76.9 17.5 %shard_map.75 = f32[4,768]{1,0:T(4,128)S(1)} custom-call(f32[8,24,256]{2,1,0:T(8,128)S(1)} %bitcast.5), custom_call_target="tpu_custom_call" | custom-call | tf_op jit(solution)/shard_map/pallas_call | solution.py:529
  94.4 0.6 copy.10
  (2 shorter events, 0.0 us)
Async XLA Ops:
  1.6 1.0 %copy-start = (bf16[40,6144]{1,0:T(8,128)(2,1)S(1)}, bf16[40,6144]{1,0:T(8,128)(2,1)}, u32[]{:S(2)}) copy-start(bf16[40,6144]{1,0:T(8,128)(2,1)} %ensemble.1) | copy-start | bytes 1474564
  2.7 0.8 copy-start.1
  3.5 0.8 copy-start.2
  4.3 0.8 copy-start.3

commit v7 on v6

--- a/solution.py
+++ b/solution.py
@@ -177,24 +177,33 @@
     taps = jnp.where(within, taps, 0.0)
     left, right = taps[:, :LANES], taps[:, LANES:]
     lane = lax.broadcasted_iota(jnp.int32, left.shape, 1)
-    none = jnp.zeros(left.shape, jnp.bfloat16)
-    upper, lower = [], []
+    middle, first, last = [], [], []
     for k in range(8):
         low = lane < 16 * k
         a, b = turn(left, 16 * k), turn(right, 16 * k)
-        middle = jnp.where(low, a, b).astype(jnp.bfloat16)
+        middle.append(jnp.where(low, a, b).astype(jnp.bfloat16))
         if k < 4:
-            upper.append(jnp.concatenate([middle, none], axis=1))
-            lower.append(jnp.concatenate([jnp.where(low, 0.0, a).astype(jnp.bfloat16), middle], axis=1))
+            first.append(jnp.where(low, 0.0, a).astype(jnp.bfloat16))
         else:
-            upper.append(jnp.concatenate([middle, jnp.where(low, b, 0.0).astype(jnp.bfloat16)], axis=1))
-            lower.append(jnp.concatenate([none, middle], axis=1))
-    return jnp.concatenate(upper + lower)
+            last.append(jnp.where(low, b, 0.0).astype(jnp.bfloat16))
+    return jnp.concatenate(middle + first + last)
 
 
 def pair_sum(row, give, take):
+    south, north = [give[:, i * LANES : (i + 1) * LANES].astype(jnp.float32) for i in range(2)]
+    low = lax.broadcasted_iota(jnp.int32, south.shape, 1) < LANES // 2
+    give = jnp.concatenate([
+        jnp.concatenate([south, jnp.where(low, north, 0.0)], axis=1),
+        jnp.concatenate([north, jnp.where(low, 0.0, south)], axis=1),
+    ]).astype(jnp.bfloat16)
     reached = jnp.dot(give, taper_tile(row), preferred_element_type=jnp.float32)
-    return jnp.sum(reached * take.astype(jnp.float32), axis=0, keepdims=True)
+    count = take.shape[0]
+    sums = [
+        jnp.sum(reached[i * count : (i + 1) * count] * take[:, i * LANES : (i + 1) * LANES].astype(jnp.float32),
+                axis=0, keepdims=True)
+        for i in range(2)
+    ]
+    return jnp.concatenate(sums, axis=1)
 
 
 def gather_kernel(

time: 95.3 us -> 95.7 us (level)
  no operation moved by 1% of the time
where the time goes in v7:
time: 95.7 us; the launch traced here: 95.3 us
  Pallas kernels  89.6 us (94%)
  local copies, waits for them, and re-layouts  4.25 us (4%)
    pallas_call x1, Pallas kernels, shards(): pl.pallas_call(functools.partial(gather_kernel, blocks), out_shape=[shape...  71.6 us
    pallas_call x1, Pallas kernels, shards(): pl.pallas_call(sum_kernel, out_shape=jax.ShapeDtypeStruct((LEVELS, column...  17.3 us
    unnamed x9, local copies, waits for them, and re-layouts  4.1 us

profile of v7, /device:TPU:1, one launch (start us, length us, event | category | flops | bytes accessed | tf_op | source)
XLA Modules:
  0.0 95.3 jit_solution(16651638409921210789)
XLA Ops:
  0.7 0.8 broadcast_multiply_fusion
  1.5 0.1 mul.20
  1.6 0.0 copy-start
  1.6 1.0 %copy-done = bf16[40,6144]{1,0:T(8,128)(2,1)S(1)} copy-done((bf16[40,6144]{1,0:T(8,128)(2,1)S(1)}, bf16[40,6144]{1,0:T(8,128)(2,1)}, u32[]{:S(2)}) %copy-start) | copy-done | bytes 491544
  2.7 0.0 copy-start.1
  2.7 0.8 copy-done.1
  3.5 0.0 copy-start.2
  3.5 0.8 copy-done.2
  4.3 0.0 copy-start.3
  4.3 0.8 copy-done.3
  5.1 71.6 %shard_map.73 = (bf16[72,40,256]{2,1,0:T(8,128)(2,1)S(1)}, bf16[48,40,256]{2,1,0:T(8,128)(2,1)S(1)}, bf16[48,40,256]{2,1,0:T(8,128)(2,1)S(1)}, bf16[24,40,256]{2...) custom-call(bf16[40,6144]{1,0:T(8,128)(2,1)S(1)} %copy-done, ...), custom_call_target="tpu_custom_call" | custom-call | tf_op jit(solution)/shard_map/pallas_call | solution.py:495
  76.7 0.7 shard_map.74
  77.4 17.3 %shard_map.75 = f32[4,768]{1,0:T(4,128)S(1)} custom-call(f32[8,24,256]{2,1,0:T(8,128)S(1)} %bitcast.5), custom_call_target="tpu_custom_call" | custom-call | tf_op jit(solution)/shard_map/pallas_call | solution.py:538
  94.7 0.6 copy.10
  (2 shorter events, 0.0 us)
Async XLA Ops:
  1.6 1.0 %copy-start = (bf16[40,6144]{1,0:T(8,128)(2,1)S(1)}, bf16[40,6144]{1,0:T(8,128)(2,1)}, u32[]{:S(2)}) copy-start(bf16[40,6144]{1,0:T(8,128)(2,1)} %ensemble.1) | copy-start | bytes 1474564
  2.7 0.8 copy-start.1
  3.5 0.8 copy-start.2
  4.3 0.8 copy-start.3

commit v8 on v7

--- a/solution.py
+++ b/solution.py
@@ -18,7 +18,7 @@
 Z = 8
 X = 4
 LANES = 128
-GROUP = 16
+GROUP = 8
 ROW_CAP = 16
 SLOTS = ((0, 7, 1), (6, 2), (5, 3), (4,))
 CAPS = (112, 80, 80, 48)
@@ -97,49 +97,47 @@
     return found
 
 
+def running(a, axis):
+    size = a.shape[axis]
+    at = lax.broadcasted_iota(jnp.int32, a.shape, axis)
+
+    def step(b, a):
+        by = lax.shift_left(jnp.int32(1), b)
+        return a + jnp.where(at >= by, pltpu.roll(a, by, axis), 0)
+
+    return lax.fori_loop(0, size.bit_length() - 1, step, a)
+
+
 def row_rank(mine):
-    rank = mine.astype(jnp.int32)
+    return running(mine.astype(jnp.int32), 1) - 1
+
+
+def pack_rows(mine, rank, arrays):
+    lanes = rank.shape[1]
     lane = lax.broadcasted_iota(jnp.int32, rank.shape, 1)
-    step = 1
-    while step < rank.shape[1]:
-        rank = rank + jnp.where(lane >= step, turn(rank, step), 0)
-        step *= 2
-    return rank - 1
-
-
-def pack_rows(mine, rank, arrays):
-    lane = lax.broadcasted_iota(jnp.int32, rank.shape, 1)
-    move = jnp.where(mine, lane - rank, 0)
-    arrays = [jnp.where(mine, a, 0) for a in arrays]
-    step = 1
-    while step < rank.shape[1]:
-        next_move = turn(move, -step)
-        arrives, leaves = (next_move & step) != 0, (move & step) != 0
-        arrays = [jnp.where(arrives, turn(a, -step), jnp.where(leaves, 0, a)) for a in arrays]
-        move = jnp.where(arrives, next_move, jnp.where(leaves, 0, move))
-        step *= 2
-    return arrays
+
+    def step(b, held):
+        by = lax.shift_left(jnp.int32(1), b)
+        move, arrays = held
+        next_move = pltpu.roll(move, lanes - by, 1)
+        arrives, leaves = (next_move & by) != 0, (move & by) != 0
+        arrays = tuple(
+            jnp.where(arrives, pltpu.roll(a, lanes - by, 1), jnp.where(leaves, jnp.zeros_like(a), a)) for a in arrays
+        )
+        return jnp.where(arrives, next_move, jnp.where(leaves, 0, move)), arrays
+
+    held = jnp.where(mine, lane - rank, 0), tuple(jnp.where(mine, a, jnp.zeros_like(a)) for a in arrays)
+    return lax.fori_loop(0, lanes.bit_length() - 1, step, held)[1]
 
 
 def group_rank(mine, group):
     rows, lanes = mine.shape
-    line = lax.broadcasted_iota(jnp.int32, (rows, lanes), 0)
-    lane = lax.broadcasted_iota(jnp.int32, (rows, lanes), 1)
     rank = jnp.zeros((rows, lanes), jnp.int32)
     for t in range(0, len(CAPS), 2):
         low, high = mine & (group == t), mine & (group == t + 1)
-        upto = low.astype(jnp.int32) + (high.astype(jnp.int32) << 16)
-        step = 1
-        while step < lanes:
-            upto = upto + jnp.where(lane >= step, turn(upto, step), 0)
-            step *= 2
+        upto = running(low.astype(jnp.int32) + (high.astype(jnp.int32) << 16), 1)
         whole = jnp.broadcast_to(upto[:, lanes - 1 :], (rows, lanes))
-        above = whole
-        step = 1
-        while step < rows:
-            above = above + jnp.where(line >= step, pltpu.roll(above, step, 0), 0)
-            step *= 2
-        upto = upto + above - whole
+        upto = upto + running(whole, 0) - whole
         rank = jnp.where(low, (upto & 0xFFFF) - 1, jnp.where(high, (upto >> 16) - 1, rank))
     return rank
 
@@ -158,14 +156,16 @@
     rows = code.shape[0]
     place_at = jnp.where(code >= USED, (code >> 15) & 1023, -1)
     lane = lax.broadcasted_iota(jnp.int32, (rows, POSITIONS), 1)
-    words = jnp.zeros((rows, POSITIONS), jnp.int32)
-    easts = jnp.zeros((rows, POSITIONS), jnp.float32)
-    norths = jnp.zeros((rows, POSITIONS), jnp.float32)
-    for j in range(ROW_CAP):
-        hit = place_at[:, j : j + 1] == lane
-        words = words + jnp.where(hit, code[:, j : j + 1], 0)
-        easts = easts + jnp.where(hit, east[:, j : j + 1], 0.0)
-        norths = norths + jnp.where(hit, north[:, j : j + 1], 0.0)
+
+    def step(j, held):
+        (place_at, *columns), sums = held
+        hit = place_at[:, 0:1] == lane
+        sums = tuple(s + jnp.where(hit, c[:, 0:1], jnp.zeros_like(s)) for s, c in zip(sums, columns))
+        return tuple(pltpu.roll(c, c.shape[1] - 1, 1) for c in (place_at, *columns)), sums
+
+    sums = tuple(jnp.zeros((rows, POSITIONS), a.dtype) for a in (code, east, north))
+    columns = tuple(a[:, :LANES] for a in (place_at, code, east, north))
+    words, easts, norths = lax.fori_loop(0, ROW_CAP, step, (columns, sums))[1]
     words, easts, norths = [jnp.sum(v, axis=0, keepdims=True) for v in (words, easts, norths)]
     return words, jnp.where(words >= USED, easts, 1e5), norths, mine & ~kept
 
@@ -212,7 +212,7 @@
     givers, refs = refs[: len(SLOTS)], refs[len(SLOTS) :]
     taking, part_out, table, found, extra, east, north = refs[:7]
     (
-        seen, counts, words, taps, words_s, row_sums, local_sem,
+        seen, counts, words, shifts, taps, words_s, row_sums, local_sem,
         z_send, z_recv, x_send, x_recv, core_send, core_recv, row_send, row_recv, col_send, col_recv,
     ) = refs[7:]
     col, z, x, core = place()
@@ -327,9 +327,14 @@
         words[...] = jnp.broadcast_to(word, words.shape)
         copy = pltpu.make_async_copy(words, words_s, local_sem.at[0])
         copy.start()
-        shift = jnp.concatenate([shift_e, shift_n, jnp.zeros((6, POSITIONS), jnp.float32)]).T
-        for at in range(0, POSITIONS, LANES):
-            taps[at : at + LANES, :] = tap_rows(shift[at : at + LANES, 0:1], shift[at : at + LANES, 1:2])
+        shifts[...] = jnp.concatenate([shift_e, shift_n, jnp.zeros((6, POSITIONS), jnp.float32)]).T
+
+        def some_taps(n, carry):
+            at = pl.ds(pl.multiple_of(n * 32, 32), 32)
+            taps[at, :] = tap_rows(shifts[at, 0:1], shifts[at, 1:2])
+            return carry
+
+        lax.fori_loop(0, POSITIONS // 32, some_taps, 0)
         receiver = slot * blocks + locals_
         rank = row_rank(left)
         table[...] = pack_rows(left, rank, [receiver | (turned << 8) | (giver << 11) | (lane << 16)])[0]
@@ -509,6 +514,7 @@
             pltpu.VMEM((owners * 8, LANES), jnp.float32),
             pltpu.VMEM((owners * 8, LANES), jnp.int32),
             pltpu.VMEM((8, POSITIONS), jnp.int32),
+            pltpu.VMEM((POSITIONS, 8), jnp.float32),
             pltpu.VMEM((POSITIONS, BLOCK), jnp.float32),
             pltpu.SMEM((8, POSITIONS), jnp.int32),
             pltpu.VMEM((POSITIONS // GROUP, GROUP, BLOCK), jnp.float32),

time: 95.7 us -> 103 us (1.076)
  Pallas kernels: 89.6 us -> 96.4 us
    pallas_call x1, Pallas kernels: 71.6 us -> 78.1 us  [shards(): pl.pallas_call(functools.partial(gather_kernel, blocks), out_shape=[shape...]
where the time goes in v8:
time: 103 us; the launch traced here: 102 us
  Pallas kernels  96.4 us (94%)
  local copies, waits for them, and re-layouts  4.25 us (4%)
    pallas_call x1, Pallas kernels, shards(): pl.pallas_call(functools.partial(gather_kernel, blocks), out_shape=[shape...  78.1 us
    pallas_call x1, Pallas kernels, shards(): pl.pallas_call(sum_kernel, out_shape=jax.ShapeDtypeStruct((LEVELS, column...  17.6 us
    unnamed x9, local copies, waits for them, and re-layouts  4.1 us

profile of v8, /device:TPU:1, one launch (start us, length us, event | category | flops | bytes accessed | tf_op | source)
XLA Modules:
  0.0 102.2 jit_solution(9000207426785021880)
XLA Ops:
  0.7 0.8 broadcast_multiply_fusion
  1.5 0.1 mul.20
  1.6 0.0 copy-start
  1.6 1.0 copy-done
  2.7 0.0 copy-start.1
  2.7 0.8 copy-done.1
  3.5 0.0 copy-start.2
  3.5 0.8 copy-done.2
  4.3 0.0 copy-start.3
  4.3 0.8 copy-done.3
  5.1 78.1 %shard_map.73 = (bf16[72,40,256]{2,1,0:T(8,128)(2,1)S(1)}, bf16[48,40,256]{2,1,0:T(8,128)(2,1)S(1)}, bf16[48,40,256]{2,1,0:T(8,128)(2,1)S(1)}, bf16[24,40,256]{2...) custom-call(bf16[40,6144]{1,0:T(8,128)(2,1)S(1)} %copy-done, ...), custom_call_target="tpu_custom_call" | custom-call | tf_op jit(solution)/shard_map/pallas_call | solution.py:500
  83.3 0.7 shard_map.74
  83.9 17.6 %shard_map.75 = f32[4,768]{1,0:T(4,128)S(1)} custom-call(f32[8,24,256]{2,1,0:T(8,128)S(1)} %bitcast.5), custom_call_target="tpu_custom_call" | custom-call | tf_op jit(solution)/shard_map/pallas_call | solution.py:544
  101.6 0.6 copy.10
  (2 shorter events, 0.0 us)
Async XLA Ops:
  1.6 1.0 %copy-start = (bf16[40,6144]{1,0:T(8,128)(2,1)S(1)}, bf16[40,6144]{1,0:T(8,128)(2,1)}, u32[]{:S(2)}) copy-start(bf16[40,6144]{1,0:T(8,128)(2,1)} %ensemble.1) | copy-start | bytes 1474564
  2.7 0.8 copy-start.1
  3.5 0.8 copy-start.2
  4.3 0.8 copy-start.3

commit v9 on v7

--- a/solution.py
+++ b/solution.py
@@ -26,6 +26,7 @@
 EARLY = 256
 POSITIONS = 384
 USED = 1 << 25
+DONE = 1 << 30
 MESH_ID = pl.DeviceIdType.MESH
 
 
@@ -130,10 +131,10 @@
         low, high = mine & (group == t), mine & (group == t + 1)
         upto = low.astype(jnp.int32) + (high.astype(jnp.int32) << 16)
         step = 1
-        while step < lanes:
+        while step < ROW_CAP:
             upto = upto + jnp.where(lane >= step, turn(upto, step), 0)
             step *= 2
-        whole = jnp.broadcast_to(upto[:, lanes - 1 :], (rows, lanes))
+        whole = jnp.broadcast_to(upto[:, ROW_CAP - 1 : ROW_CAP], (rows, lanes))
         above = whole
         step = 1
         while step < rows:
@@ -144,19 +145,26 @@
     return rank
 
 
-def make_lists(mine, slot, local, giver, turned, east, north, blocks):
-    in_row = row_rank(mine)
-    kept = mine & (in_row < ROW_CAP)
+def packed_entries(mine, slot, local, giver, turned, east, north):
+    lane = lax.broadcasted_iota(jnp.int32, mine.shape, 1)
+    code = slot | (local << 3) | (giver << 8) | (turned << 13) | (lane << 16) | (1 << 24)
+    rank = row_rank(mine)
+    return pack_rows(mine, rank, [code, east, north]), jnp.max(rank, axis=1, keepdims=True) + 1
+
+
+def make_lists(code, east, north, blocks):
+    table = code
+    code, east, north = code[:, :LANES], east[:, :LANES], north[:, :LANES]
+    kept = (code != 0) & (lax.broadcasted_iota(jnp.int32, code.shape, 1) < ROW_CAP)
+    turned = (code >> 13) & 7
     group = by_slot(turned, {t: g for g, slots in enumerate(SLOTS) for t in slots})
     rank = group_rank(kept, group)
     kept = kept & (rank < by_slot(group, dict(enumerate(CAPS))))
-    place_at = by_slot(group, dict(enumerate(STARTS))) + rank
-    giver = giver + by_slot(turned, {t: i * blocks for slots in SLOTS for i, t in enumerate(slots)})
-    code = slot | (local << 3) | (giver << 8) | (place_at << 15) | USED
-    rank = row_rank(kept)
-    code, east, north = pack_rows(kept, rank, [code, east, north])
+    place_at = jnp.where(kept, by_slot(group, dict(enumerate(STARTS))) + rank, -1)
+    giver = ((code >> 8) & 31) + by_slot(turned, {t: i * blocks for slots in SLOTS for i, t in enumerate(slots)})
+    table = jnp.concatenate([jnp.where(kept, code | DONE, code), table[:, LANES:]], axis=1)
+    code = (code & 255) | (giver << 8) | USED
     rows = code.shape[0]
-    place_at = jnp.where(code >= USED, (code >> 15) & 1023, -1)
     lane = lax.broadcasted_iota(jnp.int32, (rows, POSITIONS), 1)
     words = jnp.zeros((rows, POSITIONS), jnp.int32)
     easts = jnp.zeros((rows, POSITIONS), jnp.float32)
@@ -167,7 +175,7 @@
         easts = easts + jnp.where(hit, east[:, j : j + 1], 0.0)
         norths = norths + jnp.where(hit, north[:, j : j + 1], 0.0)
     words, easts, norths = [jnp.sum(v, axis=0, keepdims=True) for v in (words, easts, norths)]
-    return words, jnp.where(words >= USED, easts, 1e5), norths, mine & ~kept
+    return words, jnp.where(words >= USED, easts, 1e5), norths, table
 
 
 def taper_tile(row):
@@ -308,35 +316,37 @@
                 zs[way, step, c].wait_recv()
                 if step < 2 or (step == 2 and c == way):
                     zs[way, step + 1, c] = send_z(way, step + 1, c)
-    def lists():
+    def own_lists():
         for copy in col_copies:
             copy.wait_recv()
         owners = seen.shape[0] // 8
         rows = [seen[pl.ds(i, owners, stride=8), :] for i in range(4)]
-        east[...] = jnp.concatenate(rows[0:2], axis=1)
-        north[...] = jnp.concatenate(rows[2:4], axis=1)
+        shift_e, shift_n = jnp.concatenate(rows[0:2], axis=1), jnp.concatenate(rows[2:4], axis=1)
+        east[...], north[...] = shift_e, shift_n
         count = counts[pl.ds(0, owners, stride=8), :]
         count = jnp.concatenate([count, count], axis=1)
         homes = jnp.concatenate([home[pl.ds(i, owners, stride=2), :] for i in range(2)], axis=1)
         locals_ = jnp.concatenate([local[pl.ds(i, owners, stride=2), :] for i in range(2)], axis=1)
         mine, slot, giver, turned = own_entries(homes, locals_, count, z, x, core)
-        lane = lax.broadcasted_iota(jnp.int32, mine.shape, 1)
-        word, shift_e, shift_n, left = make_lists(
-            mine, slot, locals_, giver, turned, east[...], north[...], blocks
-        )
+        packed, amount = packed_entries(mine, slot, locals_, giver, turned, shift_e, shift_n)
+        found[...] = jnp.broadcast_to(amount, found.shape)
+        return packed
+
+    list_copy = pltpu.make_async_copy(words, words_s, local_sem.at[0])
+
+    def place_lists(packed):
+        word, shift_e, shift_n, entries = make_lists(*packed, blocks)
         words[...] = jnp.broadcast_to(word, words.shape)
-        copy = pltpu.make_async_copy(words, words_s, local_sem.at[0])
-        copy.start()
-        shift = jnp.concatenate([shift_e, shift_n, jnp.zeros((6, POSITIONS), jnp.float32)]).T
-        for at in range(0, POSITIONS, LANES):
-            taps[at : at + LANES, :] = tap_rows(shift[at : at + LANES, 0:1], shift[at : at + LANES, 1:2])
-        receiver = slot * blocks + locals_
-        rank = row_rank(left)
-        table[...] = pack_rows(left, rank, [receiver | (turned << 8) | (giver << 11) | (lane << 16)])[0]
-        amount = jnp.max(rank, axis=1, keepdims=True) + 1
-        found[...] = jnp.broadcast_to(amount, found.shape)
-        extra[...] = jnp.broadcast_to(jnp.max(amount, axis=0, keepdims=True), extra.shape)
-        copy.wait()
+        list_copy.start()
+        table[...] = entries
+        left = ((entries != 0) & (entries < DONE)).astype(jnp.int32)
+        left = jnp.max(jnp.max(left, axis=1, keepdims=True), axis=0, keepdims=True)
+        extra[...] = jnp.broadcast_to(left, extra.shape)
+        return jnp.concatenate([shift_e, shift_n, jnp.zeros((6, POSITIONS), jnp.float32)]).T
+
+    def some_taps(shift, c):
+        at = slice(c * LANES, (c + 1) * LANES)
+        taps[at, :] = tap_rows(shift[at, 0:1], shift[at, 1:2])
 
     def work(group, begin=0, end=None):
         first = STARTS[group] // GROUP
@@ -357,18 +367,23 @@
         lax.fori_loop(first + begin // GROUP, first + end // GROUP, some, 0)
 
     row_sums[...] = jnp.zeros_like(row_sums)
-    lists()
+    packed = own_lists()
     arrivals(0, 0)
+    shift = place_lists(packed)
     arrivals(0, 1)
+    some_taps(shift, 0)
     arrivals(1, 0)
+    list_copy.wait()
     row_arrivals(1, 1)
     for copy in cores:
         copy.wait_recv()
     work(0, 0, 48)
     arrivals(1, 1, False)
     work(0, 48)
+    some_taps(shift, 1)
     arrivals(2, 0)
     work(1)
+    some_taps(shift, 2)
     arrivals(2, 1)
     work(2)
 
@@ -410,12 +425,13 @@
         def row_step(row, carry):
             def entry_step(k, carry):
                 word = table_s[row, k]
-                receiver, turned, giver, lane = word & 255, (word >> 8) & 7, (word >> 11) & 31, word >> 16
+                receiver = (word & 7) * blocks + ((word >> 3) & 31)
+                giver, turned, lane = (word >> 8) & 31, (word >> 13) & 7, (word >> 16) & 255
                 line = tap_rows(east_s[row, lane], north_s[row, lane])
                 for ref, slots in zip(givers, SLOTS):
                     for i, t in enumerate(slots):
 
-                        @pl.when(turned == t)
+                        @pl.when((turned == t) & (word < DONE))
                         def _():
                             out[pl.ds(receiver, 1), :] += pair_sum(line, ref[i * blocks + giver], taking[receiver])
 

time: 95.7 us -> 93.4 us (0.976)
  Pallas kernels: 89.6 us -> 87.3 us
    pallas_call x1, Pallas kernels: 71.6 us -> 68.9 us  [shards(): pl.pallas_call(functools.partial(gather_kernel, blocks), out_shape=[shape...]
where the time goes in v9:
time: 93.4 us; the launch traced here: 93.1 us
  Pallas kernels  87.3 us (93%)
  local copies, waits for them, and re-layouts  4.25 us (5%)
    pallas_call x1, Pallas kernels, shards(): pl.pallas_call(functools.partial(gather_kernel, blocks), out_shape=[shape...  68.9 us
    pallas_call x1, Pallas kernels, shards(): pl.pallas_call(sum_kernel, out_shape=jax.ShapeDtypeStruct((LEVELS, column...  17.7 us
    unnamed x9, local copies, waits for them, and re-layouts  4.1 us

profile of v9, /device:TPU:1, one launch (start us, length us, event | category | flops | bytes accessed | tf_op | source)
XLA Modules:
  0.0 93.1 jit_solution(15743907005307192133)
XLA Ops:
  0.7 0.8 broadcast_multiply_fusion
  1.5 0.1 mul.20
  1.6 0.0 copy-start
  1.6 1.0 %copy-done = bf16[40,6144]{1,0:T(8,128)(2,1)S(1)} copy-done((bf16[40,6144]{1,0:T(8,128)(2,1)S(1)}, bf16[40,6144]{1,0:T(8,128)(2,1)}, u32[]{:S(2)}) %copy-start) | copy-done | bytes 491544
  2.7 0.0 copy-start.1
  2.7 0.8 copy-done.1
  3.5 0.0 copy-start.2
  3.5 0.8 copy-done.2
  4.3 0.0 copy-start.3
  4.3 0.8 copy-done.3
  5.1 68.9 %shard_map.73 = (bf16[72,40,256]{2,1,0:T(8,128)(2,1)S(1)}, bf16[48,40,256]{2,1,0:T(8,128)(2,1)S(1)}, bf16[48,40,256]{2,1,0:T(8,128)(2,1)S(1)}, bf16[24,40,256]{2...) custom-call(bf16[40,6144]{1,0:T(8,128)(2,1)S(1)} %copy-done, ...), custom_call_target="tpu_custom_call" | custom-call | tf_op jit(solution)/shard_map/pallas_call | solution.py:511
  74.1 0.7 shard_map.74
  74.7 17.7 %shard_map.75 = f32[4,768]{1,0:T(4,128)S(1)} custom-call(f32[8,24,256]{2,1,0:T(8,128)S(1)} %bitcast.5), custom_call_target="tpu_custom_call" | custom-call | tf_op jit(solution)/shard_map/pallas_call | solution.py:554
  92.5 0.6 copy.10
  (2 shorter events, 0.0 us)
Async XLA Ops:
  1.6 1.0 %copy-start = (bf16[40,6144]{1,0:T(8,128)(2,1)S(1)}, bf16[40,6144]{1,0:T(8,128)(2,1)}, u32[]{:S(2)}) copy-start(bf16[40,6144]{1,0:T(8,128)(2,1)} %ensemble.1) | copy-start | bytes 1474564
  2.7 0.8 copy-start.1
  3.5 0.8 copy-start.2
  4.3 0.8 copy-start.3

commit v10 on v9

--- a/solution.py
+++ b/solution.py
@@ -215,7 +215,7 @@
 
 
 def gather_kernel(
-    blocks, ensemble, control, small, live, home, local, *refs,
+    blocks, ensemble, control, small, live, named, *refs,
 ):
     givers, refs = refs[: len(SLOTS)], refs[len(SLOTS) :]
     taking, part_out, table, found, extra, east, north = refs[:7]
@@ -325,8 +325,8 @@
         east[...], north[...] = shift_e, shift_n
         count = counts[pl.ds(0, owners, stride=8), :]
         count = jnp.concatenate([count, count], axis=1)
-        homes = jnp.concatenate([home[pl.ds(i, owners, stride=2), :] for i in range(2)], axis=1)
-        locals_ = jnp.concatenate([local[pl.ds(i, owners, stride=2), :] for i in range(2)], axis=1)
+        names = jnp.concatenate([named[pl.ds(i, owners, stride=2), :] for i in range(2)], axis=1)
+        homes, locals_ = names & 63, names >> 6
         mine, slot, giver, turned = own_entries(homes, locals_, count, z, x, core)
         packed, amount = packed_entries(mine, slot, locals_, giver, turned, shift_e, shift_n)
         found[...] = jnp.broadcast_to(amount, found.shape)
@@ -450,7 +450,9 @@
     def mem_peer(step):
         return {"mem": lax.rem(mem + step, mems)}
 
-    greet([row_peer(z, x, core, s) for s in range(1, XC)] + [mem_peer(s) for s in range(1, mems)])()
+    entered = greet([row_peer(z, x, core, s) for s in range(1, XC)] + [mem_peer(s) for s in range(1, mems)])
+    mine[...] = jnp.zeros_like(mine)
+    entered()
     copies = []
     for s in range(1, XC):
         copy = pltpu.make_async_remote_copy(
@@ -461,14 +463,14 @@
         copy.start()
         copies.append(copy)
     summed = part[0]
-    for s in range(1, XC):
-        copies[s - 1].wait()
+    for copy in copies:
+        copy.wait_recv()
+    first = list(copies)
     for s in range(1, XC):
         summed = summed + rows_in[s]
     each = summed.shape[0] // mems
     for m in range(mems):
         mine[m, :each, :] = summed[m * each : (m + 1) * each, :]
-        mine[m, each:, :] = jnp.zeros((mine.shape[1] - each, BLOCK), jnp.float32)
     pieces[mem] = mine[mem]
     copies = []
     for s in range(1, mems):
@@ -480,7 +482,9 @@
         copy.start()
         copies.append(copy)
     for copy in copies:
-        copy.wait()
+        copy.wait_recv()
+    for copy in first + copies:
+        copy.wait_send()
     for l in range(LEVELS):
         first = l * (mems // LEVELS)
         both = pieces[first]
@@ -501,8 +505,7 @@
     both = (pair_shift[:, :, None] * sign).reshape(2, entries)
     small = jnp.concatenate([both.reshape(4, LANES), jnp.zeros((4, LANES), jnp.float32)])
     live = jnp.broadcast_to(pair_count[:, None], (8, LANES))
-    home = pair_home.reshape(-1, LANES)
-    local = pair_local.reshape(-1, LANES)
+    named = pair_home.reshape(-1, LANES) | (pair_local.reshape(-1, LANES) << 6)
     smem = pl.BlockSpec(memory_space=pltpu.SMEM)
     vmem = pl.BlockSpec(memory_space=pltpu.VMEM)
     dma = pltpu.SemaphoreType.DMA
@@ -519,7 +522,7 @@
             shape((owners, entries), jnp.float32),
             shape((owners, entries), jnp.float32),
         ],
-        in_specs=[vmem] * 6,
+        in_specs=[vmem] * 5,
         out_specs=[vmem] * (len(SLOTS) + 7),
         scratch_shapes=[
             pltpu.VMEM((owners * 8, LANES), jnp.float32),
@@ -535,7 +538,7 @@
         compiler_params=pltpu.CompilerParams(
             collective_id=0, has_side_effects=True, vmem_limit_bytes=28 * 1024 * 1024
         ),
-    )(ensemble, control, small, live, home, local)
+    )(ensemble, control, small, live, named)
 
     part = pl.pallas_call(
         functools.partial(extra_kernel, blocks),

time: 93.4 us -> 92.4 us (0.989)
  local copies, waits for them, and re-layouts: 4.25 us -> 2.57 us
    unnamed x9 -> x5, local copies, waits for them, and re-layouts: 4.1 us -> 2.43 us
where the time goes in v10:
time: 92.4 us; the launch traced here: 92.1 us
  Pallas kernels  87.2 us (94%)
  local copies, waits for them, and re-layouts  2.57 us (3%)
  other arithmetic  1.68 us (2%)
    pallas_call x1, Pallas kernels, shards(): pl.pallas_call(functools.partial(gather_kernel, blocks), out_shape=[shape...  68.9 us
    pallas_call x1, Pallas kernels, shards(): pl.pallas_call(sum_kernel, out_shape=jax.ShapeDtypeStruct((LEVELS, column...  17.6 us
    unnamed x5, local copies, waits for them, and re-layouts  2.43 us

profile of v10, /device:TPU:1, one launch (start us, length us, event | category | flops | bytes accessed | tf_op | source)
XLA Modules:
  0.0 92.1 jit_solution(10076927759262180796)
XLA Ops:
  0.7 0.9 bitcast_or_fusion.named
  1.5 0.8 broadcast_multiply_fusion
  2.3 0.1 mul.20
  2.5 0.0 copy-start
  2.5 1.0 %copy-done = bf16[40,6144]{1,0:T(8,128)(2,1)S(1)} copy-done((bf16[40,6144]{1,0:T(8,128)(2,1)S(1)}, bf16[40,6144]{1,0:T(8,128)(2,1)}, u32[]{:S(2)}) %copy-start) | copy-done | bytes 491544
  3.5 0.0 copy-start.1
  3.5 0.8 copy-done.1
  4.3 68.9 %shard_map.73 = (bf16[72,40,256]{2,1,0:T(8,128)(2,1)S(1)}, bf16[48,40,256]{2,1,0:T(8,128)(2,1)S(1)}, bf16[48,40,256]{2,1,0:T(8,128)(2,1)S(1)}, bf16[24,40,256]{2...) custom-call(bf16[40,6144]{1,0:T(8,128)(2,1)S(1)} %copy-done, ...), custom_call_target="tpu_custom_call" | custom-call | tf_op jit(solution)/shard_map/pallas_call | solution.py:514
  73.3 0.7 shard_map.74
  73.9 17.6 %shard_map.75 = f32[4,768]{1,0:T(4,128)S(1)} custom-call(f32[8,24,256]{2,1,0:T(8,128)S(1)} %bitcast.6), custom_call_target="tpu_custom_call" | custom-call | tf_op jit(solution)/shard_map/pallas_call | solution.py:557
  91.5 0.6 copy.10
  (2 shorter events, 0.0 us)
Async XLA Ops:
  2.5 1.0 %copy-start = (bf16[40,6144]{1,0:T(8,128)(2,1)S(1)}, bf16[40,6144]{1,0:T(8,128)(2,1)}, u32[]{:S(2)}) copy-start(bf16[40,6144]{1,0:T(8,128)(2,1)} %ensemble.1) | copy-start | bytes 1474564
  3.5 0.8 copy-start.1

commit v11 on v10

--- a/solution.py
+++ b/solution.py
@@ -18,11 +18,11 @@
 Z = 8
 X = 4
 LANES = 128
-GROUP = 16
+GROUP = 8
 ROW_CAP = 16
 SLOTS = ((0, 7, 1), (6, 2), (5, 3), (4,))
-CAPS = (112, 80, 80, 48)
-STARTS = (0, 112, 192, 272)
+CAPS = (104, 72, 72, 40)
+STARTS = (0, 104, 176, 256)
 EARLY = 256
 POSITIONS = 384
 USED = 1 << 25

time: 92.4 us -> 92 us (level)
  no operation moved by 1% of the time
where the time goes in v11:
time: 92 us; the launch traced here: 91.7 us
  Pallas kernels  86.7 us (94%)
  local copies, waits for them, and re-layouts  2.57 us (3%)
  other arithmetic  1.68 us (2%)
    pallas_call x1, Pallas kernels, shards(): pl.pallas_call(functools.partial(gather_kernel, blocks), out_shape=[shape...  68.3 us
    pallas_call x1, Pallas kernels, shards(): pl.pallas_call(sum_kernel, out_shape=jax.ShapeDtypeStruct((LEVELS, column...  17.8 us
    unnamed x5, local copies, waits for them, and re-layouts  2.43 us

profile of v11, /device:TPU:1, one launch (start us, length us, event | category | flops | bytes accessed | tf_op | source)
XLA Modules:
  0.0 91.7 jit_solution(2394656967901264643)
XLA Ops:
  0.7 0.9 bitcast_or_fusion.named
  1.5 0.8 broadcast_multiply_fusion
  2.3 0.1 mul.20
  2.5 0.0 copy-start
  2.5 1.0 %copy-done = bf16[40,6144]{1,0:T(8,128)(2,1)S(1)} copy-done((bf16[40,6144]{1,0:T(8,128)(2,1)S(1)}, bf16[40,6144]{1,0:T(8,128)(2,1)}, u32[]{:S(2)}) %copy-start) | copy-done | bytes 491544
  3.5 0.0 copy-start.1
  3.5 0.8 copy-done.1
  4.3 68.3 %shard_map.73 = (bf16[72,40,256]{2,1,0:T(8,128)(2,1)S(1)}, bf16[48,40,256]{2,1,0:T(8,128)(2,1)S(1)}, bf16[48,40,256]{2,1,0:T(8,128)(2,1)S(1)}, bf16[24,40,256]{2...) custom-call(bf16[40,6144]{1,0:T(8,128)(2,1)S(1)} %copy-done, ...), custom_call_target="tpu_custom_call" | custom-call | tf_op jit(solution)/shard_map/pallas_call | solution.py:514
  72.7 0.7 shard_map.74
  73.3 17.8 %shard_map.75 = f32[4,768]{1,0:T(4,128)S(1)} custom-call(f32[8,24,256]{2,1,0:T(8,128)S(1)} %bitcast.6), custom_call_target="tpu_custom_call" | custom-call | tf_op jit(solution)/shard_map/pallas_call | solution.py:557
  91.1 0.6 copy.10
  (2 shorter events, 0.0 us)
Async XLA Ops:
  2.5 1.0 %copy-start = (bf16[40,6144]{1,0:T(8,128)(2,1)S(1)}, bf16[40,6144]{1,0:T(8,128)(2,1)}, u32[]{:S(2)}) copy-start(bf16[40,6144]{1,0:T(8,128)(2,1)} %ensemble.1) | copy-start | bytes 1474564
  3.5 0.8 copy-start.1
